TPU v7x, 32 devices: a whole 2x2x4 slice. The times are simulated.
32 devices in a mesh: dp: 4 (over z), fsdp: 8 (over y, x, core).
Axes of the slice: x: 2, y: 2, z: 4, core: 2. Of those that a mesh axis runs over, the one named last changes fastest.
Arguments:
- tokens: bfloat16 [32768, 768], P(('dp', 'fsdp')), may hold values from -6 to 6
- token_ids: int32 [32768], P(('dp', 'fsdp')), may hold values from 0 to 8007
- lengths: int32 [32], P(('dp', 'fsdp')), may hold values from 1 to 1024, 20480 in all
- hash_table: int32 [8008], replicated, may hold values from 0 to 3
- w_qkv: bfloat16 [768, 2304], P(('dp', 'fsdp')), may hold values from -0.21875 to 0.21875
- w_attn_out: bfloat16 [768, 768], P(('dp', 'fsdp')), may hold values from -1.75 to 1.75
- norm_gains: bfloat16 [768, 2], P(('dp', 'fsdp')), may hold values from 0.5 to 1.5
- norm_biases: bfloat16 [768, 2], P(('dp', 'fsdp')), may hold values from -1.5 to 1.5
- w_in: bfloat16 [3072, 3072], P(('dp', 'fsdp')), may hold values from -0.21875 to 0.21875
- w_out: bfloat16 [12288, 768], P(('dp', 'fsdp')), may hold values from -0.109375 to 0.109375
- cotangent: bfloat16 [32768, 768], P(('dp', 'fsdp')), may hold values from -6 to 6
Outputs:
- layer_out: bfloat16 [32768, 768], P(('dp', 'fsdp'))
- grad_tokens: float32 [32768, 768], P(('dp', 'fsdp'))
- grad_w_qkv: float32 [768, 2304], P(('dp', 'fsdp'))
- grad_w_attn_out: float32 [768, 768], P(('dp', 'fsdp'))
- grad_norm_gains: float32 [768, 2], P(('dp', 'fsdp'))
- grad_norm_biases: float32 [768, 2], P(('dp', 'fsdp'))
- grad_w_in: float32 [3072, 3072], P(('dp', 'fsdp'))
- grad_w_out: float32 [12288, 768], P(('dp', 'fsdp'))
- expert_counts: int32 [4], replicated
Inputs may be any that keep to these rules, and one draw needn't show every extreme that they name: `lengths`: every sequence has at least one used token and one sequence of each draw uses all 1024 slots.
All inputs are finite; a program needn't handle non-finite values. No bound on the sum of `lengths` on one device may be relied on, other than what follows from the above.
Results may differ from a plain program's by a relative error of at most 0.0094.
Values may be sent and summed in bfloat16 or wider, within the bound.
A program may use at most 512 MiB of HBM per device.

v0:
```python
import jax
import jax.numpy as jnp
from jax import lax
from jax.sharding import PartitionSpec as P

D = 768
HEADS = 12
HEAD_DIM = 64
EXPERTS = 4
BLOCK = 128


EPSILON = 1e-05
NEGATIVE = -1e30


def layer_stats(values):
    average = jnp.mean(values, axis=-1, keepdims=True)
    centred = values - average
    scaled = lax.rsqrt(jnp.mean(centred * centred, axis=-1, keepdims=True) + EPSILON)
    return (centred * scaled, scaled)


def norm_backward(grad_normed, normal, scaled, gain_col):
    grad_scaled = grad_normed * gain_col
    first_mean = jnp.mean(grad_scaled, axis=-1, keepdims=True)
    second_mean = jnp.mean(grad_scaled * normal, axis=-1, keepdims=True)
    return scaled * (grad_scaled - first_mean - normal * second_mean)


def head_groups(heads):
    group_width = 4
    return [(start, start + group_width) for start in range(0, heads, group_width)]


def allowed_keys(length, seq_len):
    places = jnp.arange(seq_len, dtype=jnp.int32)
    return (places[None, :] <= places[:, None]) & (places[None, :] < length)


def masked_scores(query_part, key_part, allowed):
    scale = query_part.shape[-1] ** (-0.5)
    raw = (
        jnp.einsum("qhd,khd->hqk", query_part, key_part, preferred_element_type=jnp.float32) * scale
    )
    return jnp.where(allowed[None], raw, NEGATIVE)


def attention_forward(entry):
    queries, keys, values, length = entry
    allowed = allowed_keys(length, queries.shape[0])
    mixed_parts = []
    total_parts = []
    for start, finish in head_groups(queries.shape[1]):
        scores = masked_scores(queries[:, start:finish], keys[:, start:finish], allowed)
        highest = jnp.max(scores, axis=-1, keepdims=True)
        totals = highest + jnp.log(jnp.sum(jnp.exp(scores - highest), axis=-1, keepdims=True))
        weights = jnp.exp(scores - totals).astype(jnp.bfloat16)
        mixed_parts.append(
            jnp.einsum(
                "hqk,khd->qhd", weights, values[:, start:finish], preferred_element_type=jnp.float32
            ).astype(jnp.bfloat16)
        )
        total_parts.append(totals[..., 0])
    return (jnp.concatenate(mixed_parts, axis=1), jnp.concatenate(total_parts, axis=0))


def attention_backward(entry):
    queries, keys, values, totals, grad_mixed, length = entry
    allowed = allowed_keys(length, queries.shape[0])
    scale = queries.shape[-1] ** (-0.5)
    query_parts, key_parts, value_parts = ([], [], [])
    for start, finish in head_groups(queries.shape[1]):
        scores = masked_scores(queries[:, start:finish], keys[:, start:finish], allowed)
        weights = jnp.exp(scores - totals[start:finish][..., None])
        grad_weights = jnp.einsum(
            "qhd,khd->hqk",
            grad_mixed[:, start:finish],
            values[:, start:finish],
            preferred_element_type=jnp.float32,
        )
        inner_sum = jnp.sum(grad_weights * weights, axis=-1, keepdims=True)
        grad_scores = (weights * (grad_weights - inner_sum)).astype(jnp.bfloat16)
        value_parts.append(
            jnp.einsum(
                "hqk,qhd->khd",
                weights.astype(jnp.bfloat16),
                grad_mixed[:, start:finish],
                preferred_element_type=jnp.float32,
            )
        )
        query_parts.append(
            jnp.einsum(
                "hqk,khd->qhd",
                grad_scores,
                keys[:, start:finish],
                preferred_element_type=jnp.float32,
            )
            * scale
        )
        key_parts.append(
            jnp.einsum(
                "hqk,qhd->khd",
                grad_scores,
                queries[:, start:finish],
                preferred_element_type=jnp.float32,
            )
            * scale
        )
    return (
        jnp.concatenate(query_parts, axis=1),
        jnp.concatenate(key_parts, axis=1),
        jnp.concatenate(value_parts, axis=1),
    )


def segment_table(group_ends, total_rows, block_rows):
    block_count = total_rows // block_rows
    block_starts = jnp.arange(block_count, dtype=jnp.int32) * block_rows
    points = jnp.sort(jnp.concatenate([block_starts, group_ends]))
    finishes = jnp.concatenate([points[1:], jnp.full((1,), total_rows, jnp.int32)])
    blocks = jnp.minimum(points // block_rows, block_count - 1)
    owners = jnp.sum((group_ends[None, :] <= points[:, None]).astype(jnp.int32), axis=1)
    active = (finishes > points) & (owners < group_ends.shape[0])
    owners = jnp.minimum(owners, group_ends.shape[0] - 1)
    return (points, finishes, blocks, owners, active)


def expert_forward(sorted_rows, inner_all, outer_all, table, block_rows):
    model_width = sorted_rows.shape[1]
    hidden_width = inner_all.shape[1]

    def visit(state, entry):
        start, finish, block_id, owner, live = entry

        def compute(inner_state):
            pre_all, result_all = inner_state
            base = block_id * block_rows
            rows_here = lax.dynamic_slice_in_dim(sorted_rows, base, block_rows, 0)
            inner = lax.dynamic_slice_in_dim(inner_all, owner * model_width, model_width, 0)
            outer = lax.dynamic_slice_in_dim(outer_all, owner * hidden_width, hidden_width, 0)
            places = base + jnp.arange(block_rows, dtype=jnp.int32)
            inside = ((places >= start) & (places < finish))[:, None]
            pre = jnp.dot(rows_here, inner, preferred_element_type=jnp.float32)
            result = jnp.dot(
                jax.nn.gelu(pre).astype(jnp.bfloat16), outer, preferred_element_type=jnp.float32
            )
            old_pre = lax.dynamic_slice_in_dim(pre_all, base, block_rows, 0)
            old_result = lax.dynamic_slice_in_dim(result_all, base, block_rows, 0)
            pre_all = lax.dynamic_update_slice_in_dim(
                pre_all, jnp.where(inside, pre, old_pre), base, 0
            )
            result_all = lax.dynamic_update_slice_in_dim(
                result_all, jnp.where(inside, result, old_result), base, 0
            )
            return (pre_all, result_all)

        return (lax.cond(live, compute, lambda same: same, state), None)

    start_state = (
        jnp.zeros((sorted_rows.shape[0], hidden_width), jnp.float32),
        jnp.zeros((sorted_rows.shape[0], model_width), jnp.float32),
    )
    final_state, _ = lax.scan(visit, start_state, table)
    return final_state


def expert_backward(sorted_rows, pre_all, grad_sorted, inner_all, outer_all, table, block_rows):
    model_width = sorted_rows.shape[1]
    hidden_width = inner_all.shape[1]

    def visit(state, entry):
        start, finish, block_id, owner, live = entry

        def compute(inner_state):
            grad_rows, grad_inner, grad_outer = inner_state
            base = block_id * block_rows
            rows_here = lax.dynamic_slice_in_dim(sorted_rows, base, block_rows, 0)
            pre = lax.dynamic_slice_in_dim(pre_all, base, block_rows, 0)
            inner = lax.dynamic_slice_in_dim(inner_all, owner * model_width, model_width, 0)
            outer = lax.dynamic_slice_in_dim(outer_all, owner * hidden_width, hidden_width, 0)
            places = base + jnp.arange(block_rows, dtype=jnp.int32)
            inside = ((places >= start) & (places < finish))[:, None]
            grad_block = jnp.where(
                inside,
                lax.dynamic_slice_in_dim(grad_sorted, base, block_rows, 0),
                jnp.zeros((), jnp.bfloat16),
            )
            activated, gelu_pull = jax.vjp(jax.nn.gelu, pre)
            outer_piece = jnp.einsum(
                "tf,td->fd",
                activated.astype(jnp.bfloat16),
                grad_block,
                preferred_element_type=jnp.float32,
            )
            grad_act = jnp.einsum(
                "td,fd->tf", grad_block, outer, preferred_element_type=jnp.float32
            )
            grad_pre = gelu_pull(grad_act)[0].astype(jnp.bfloat16)
            inner_piece = jnp.einsum(
                "td,tf->df", rows_here, grad_pre, preferred_element_type=jnp.float32
            )
            rows_piece = jnp.einsum(
                "tf,df->td", grad_pre, inner, preferred_element_type=jnp.float32
            )
            old_rows = lax.dynamic_slice_in_dim(grad_rows, base, block_rows, 0)
            grad_rows = lax.dynamic_update_slice_in_dim(grad_rows, old_rows + rows_piece, base, 0)
            old_inner = lax.dynamic_slice_in_dim(grad_inner, owner * model_width, model_width, 0)
            grad_inner = lax.dynamic_update_slice_in_dim(
                grad_inner, old_inner + inner_piece, owner * model_width, 0
            )
            old_outer = lax.dynamic_slice_in_dim(grad_outer, owner * hidden_width, hidden_width, 0)
            grad_outer = lax.dynamic_update_slice_in_dim(
                grad_outer, old_outer + outer_piece, owner * hidden_width, 0
            )
            return (grad_rows, grad_inner, grad_outer)

        return (lax.cond(live, compute, lambda same: same, state), None)

    start_state = (
        jnp.zeros(sorted_rows.shape, jnp.float32),
        jnp.zeros(inner_all.shape, jnp.float32),
        jnp.zeros(outer_all.shape, jnp.float32),
    )
    final_state, _ = lax.scan(visit, start_state, table)
    return final_state


def body(
    tokens,
    token_ids,
    lengths,
    hash_table,
    w_qkv,
    w_attn_out,
    norm_gains,
    norm_biases,
    w_in,
    w_out,
    cotangent,
):
    rows_count = tokens.shape[0]
    seq_count = lengths.shape[0]
    seq_len = rows_count // seq_count
    model_width = D
    expert_total = EXPERTS
    qkv_full, proj_full, gains_full, biases_full = (
        lax.all_gather(w_qkv, ("dp", "fsdp"), axis=0, tiled=True),
        lax.all_gather(w_attn_out, ("dp", "fsdp"), axis=0, tiled=True),
        lax.all_gather(norm_gains, ("dp", "fsdp"), axis=0, tiled=True),
        lax.all_gather(norm_biases, ("dp", "fsdp"), axis=0, tiled=True),
    )
    gains_f = gains_full.astype(jnp.float32)
    biases_f = biases_full.astype(jnp.float32)
    inputs = tokens.astype(jnp.float32)
    normal_one, scaled_one = layer_stats(inputs)
    first_in = (normal_one * gains_f[:, 0] + biases_f[:, 0]).astype(jnp.bfloat16)
    qkv_low = jnp.dot(first_in, qkv_full, preferred_element_type=jnp.float32).astype(jnp.bfloat16)
    packed = qkv_low.reshape(seq_count, seq_len, 3, HEADS, HEAD_DIM)
    queries = packed[:, :, 0]
    keys = packed[:, :, 1]
    values = packed[:, :, 2]
    mixed, totals = lax.map(attention_forward, (queries, keys, values, lengths))
    mixed_flat = mixed.reshape(rows_count, model_width)
    hidden = inputs + jnp.dot(mixed_flat, proj_full, preferred_element_type=jnp.float32)
    normal_two, scaled_two = layer_stats(hidden)
    second_in = (normal_two * gains_f[:, 1] + biases_f[:, 1]).astype(jnp.bfloat16)
    places = jnp.arange(rows_count, dtype=jnp.int32) % seq_len
    used = places < jnp.repeat(lengths, seq_len, total_repeat_length=rows_count)
    expert_ids = jnp.where(used, hash_table[token_ids], expert_total)
    matches = (expert_ids[:, None] == jnp.arange(expert_total, dtype=jnp.int32)[None, :]).astype(
        jnp.int32
    )
    local_counts = jnp.sum(matches, axis=0)
    expert_counts = lax.psum(local_counts, ("dp", "fsdp"))
    ordering = jnp.argsort(expert_ids, stable=True)
    inverse = (
        jnp.zeros((rows_count,), jnp.int32)
        .at[ordering]
        .set(jnp.arange(rows_count, dtype=jnp.int32))
    )
    group_ends = jnp.cumsum(local_counts)
    table = segment_table(group_ends, rows_count, BLOCK)
    inner_all, outer_all = (
        lax.all_gather(w_in, ("dp", "fsdp"), axis=0, tiled=True),
        lax.all_gather(w_out, ("dp", "fsdp"), axis=0, tiled=True),
    )
    sorted_rows = second_in[ordering]
    pre_all, result_sorted = expert_forward(sorted_rows, inner_all, outer_all, table, BLOCK)
    layer_out = (hidden + result_sorted[inverse]).astype(jnp.bfloat16)
    grad_out = cotangent.astype(jnp.float32)
    grad_sorted = cotangent[ordering]
    inner_back, outer_back = (
        lax.all_gather(w_in, ("dp", "fsdp"), axis=0, tiled=True),
        lax.all_gather(w_out, ("dp", "fsdp"), axis=0, tiled=True),
    )
    grad_rows_sorted, grad_inner, grad_outer = expert_backward(
        sorted_rows, pre_all, grad_sorted, inner_back, outer_back, table, BLOCK
    )
    grad_w_in, grad_w_out = (
        lax.psum_scatter(grad_inner, ("dp", "fsdp"), scatter_dimension=0, tiled=True),
        lax.psum_scatter(grad_outer, ("dp", "fsdp"), scatter_dimension=0, tiled=True),
    )
    grad_second = grad_rows_sorted[inverse]
    gain_two = jnp.sum(grad_second * normal_two, axis=0)
    bias_two = jnp.sum(grad_second, axis=0)
    grad_hidden = grad_out + norm_backward(grad_second, normal_two, scaled_two, gains_f[:, 1])
    grad_branch = grad_hidden.astype(jnp.bfloat16)
    qkv_back, proj_back = (
        lax.all_gather(w_qkv, ("dp", "fsdp"), axis=0, tiled=True),
        lax.all_gather(w_attn_out, ("dp", "fsdp"), axis=0, tiled=True),
    )
    grad_proj = jnp.einsum("td,te->de", mixed_flat, grad_branch, preferred_element_type=jnp.float32)
    grad_mixed = jnp.einsum(
        "te,de->td", grad_branch, proj_back, preferred_element_type=jnp.float32
    ).astype(jnp.bfloat16)
    grad_mixed = grad_mixed.reshape(seq_count, seq_len, HEADS, HEAD_DIM)
    grad_queries, grad_keys, grad_values = lax.map(
        attention_backward, (queries, keys, values, totals, grad_mixed, lengths)
    )
    grad_qkv = (
        jnp.stack([grad_queries, grad_keys, grad_values], axis=2)
        .reshape(rows_count, 3 * model_width)
        .astype(jnp.bfloat16)
    )
    grad_qkv_w = jnp.einsum("td,te->de", first_in, grad_qkv, preferred_element_type=jnp.float32)
    grad_first = jnp.einsum("te,de->td", grad_qkv, qkv_back, preferred_element_type=jnp.float32)
    gain_one = jnp.sum(grad_first * normal_one, axis=0)
    bias_one = jnp.sum(grad_first, axis=0)
    grad_tokens = grad_hidden + norm_backward(grad_first, normal_one, scaled_one, gains_f[:, 0])
    grad_gains = jnp.stack([gain_one, gain_two], axis=1)
    grad_biases = jnp.stack([bias_one, bias_two], axis=1)
    grad_w_qkv, grad_w_attn_out, grad_norm_gains, grad_norm_biases = (
        lax.psum_scatter(grad_qkv_w, ("dp", "fsdp"), scatter_dimension=0, tiled=True),
        lax.psum_scatter(grad_proj, ("dp", "fsdp"), scatter_dimension=0, tiled=True),
        lax.psum_scatter(grad_gains, ("dp", "fsdp"), scatter_dimension=0, tiled=True),
        lax.psum_scatter(grad_biases, ("dp", "fsdp"), scatter_dimension=0, tiled=True),
    )
    return (
        layer_out,
        grad_tokens,
        grad_w_qkv,
        grad_w_attn_out,
        grad_norm_gains,
        grad_norm_biases,
        grad_w_in,
        grad_w_out,
        expert_counts,
    )


def solution(mesh):
    placed = (
        P(("dp", "fsdp"), None),
        P(("dp", "fsdp")),
        P(("dp", "fsdp")),
        P(),
        P(("dp", "fsdp"), None),
        P(("dp", "fsdp"), None),
        P(("dp", "fsdp"), None),
        P(("dp", "fsdp"), None),
        P(("dp", "fsdp"), None),
        P(("dp", "fsdp"), None),
        P(("dp", "fsdp"), None),
    )
    return jax.shard_map(
        body,
        mesh=mesh,
        in_specs=placed,
        out_specs=(
            P(("dp", "fsdp"), None),
            P(("dp", "fsdp"), None),
            P(("dp", "fsdp"), None),
            P(("dp", "fsdp"), None),
            P(("dp", "fsdp"), None),
            P(("dp", "fsdp"), None),
            P(("dp", "fsdp"), None),
            P(("dp", "fsdp"), None),
            P(),
        ),
        check_vma=False,
    )
```

profile of v0, /device:TPU:0, one launch (start us, length us, event | category | flops | bytes accessed | tf_op | source)
XLA Modules:
  0.0 2097.3 jit_solution(2352631872196736443)
XLA Ops:
  11.9 43.0 %all-gather = bf16[32,24,2]{1,2,0:T(2,128)(2,1)S(1)} all-gather(bf16[1,24,2]{1,2,0:T(2,128)(2,1)S(1)} %bitcast.136), channel_id=1, replica_groups=mesh['dp'=4,'fsdp'=8] {'dp','fsdp'}, dimensions={0}, use_global_device_ids=true | all-gather | bytes 3168 | tf_op jit(solution)/shard_map/all_gather | solution.py:250
  55.3 36.4 %all-gather.1 = bf16[32,24,2]{1,2,0:T(2,128)(2,1)S(1)} all-gather(bf16[1,24,2]{1,2,0:T(2,128)(2,1)S(1)} %bitcast.137), channel_id=1, replica_groups=mesh['dp'=4,'fsdp'=8] {'dp','fsdp'}, dimensions={0}, use_global_device_ids=true | all-gather | bytes 3168 | tf_op jit(solution)/shard_map/all_gather | solution.py:251
  118.4 8.1 convolution_convert_fusion
  136.7 8.5 fusion.106
  152.7 20.2 exponential_reduce_fusion.2
  172.9 13.5 exponential_reduce_fusion.1
  186.4 10.0 fusion.91
  196.4 12.6 fusion.92
  209.0 10.1 fusion.93
  230.9 27.1 %all-gather.11.cloned.1.call-done = bf16[3072,3072]{1,0:T(8,128)(2,1)} async-done(((bf16[96,3072]{1,0:T(8,128)(2,1)}), bf16[3072,3072]{1,0:T(8,128)(2,1)}) %all-gather.11.cloned.1.call-update) | async-done | bytes 18874384 | tf_op jit(solution)/shard_map/all_gather | solution.py:285
  258.0 125.6 %all-gather.13.cloned.1.call-done = bf16[12288,768]{1,0:T(8,128)(2,1)} async-done(((bf16[384,768]{1,0:T(8,128)(2,1)}), bf16[12288,768]{1,0:T(8,128)(2,1)}) %all-gather.13.cloned.1.call-update) | async-done | bytes 18874384 | tf_op jit(solution)/shard_map/all_gather | solution.py:286
  389.8 149.6 %while.6 = (s32[]{:T(128)}, f32[1024,3072]{1,0:T(8,128)}, f32[1024,768]{1,0:T(8,128)S(1)}, pred[12]{0:T(512)(128)(4,1)S(1)}, s32[12]{0:T(128)S(1)}, /*index=5*/s...) while((s32[]{:T(128)}, f32[1024,3072]{1,0:T(8,128)}, ...), condition=%wide.region_18.19_spmd, body=%wide.region_15.18_spmd.sunk | while | flops 1211990528 | bytes 16714438 | solution.py:164
  391.1 15.0 conditional.4
  407.3 14.9 conditional.4
  423.5 14.9 conditional.4
  439.7 14.9 conditional.4
  455.9 14.9 conditional.4
  472.1 14.9 conditional.4
  488.3 14.9 conditional.4
  504.4 14.9 conditional.4
  520.6 14.9 conditional.4
  539.4 12.9 broadcast_in_dim.182
  552.4 12.4 broadcast_in_dim.183
  565.0 322.4 %while.7 = (s32[]{:T(128)}, f32[1024,768]{1,0:T(8,128)S(1)}, f32[3072,3072]{1,0:T(8,128)}, f32[12288,768]{1,0:T(8,128)}, pred[12]{0:T(512)(128)(4,1)S(1)}, /*ind...) while((s32[]{:T(128)}, f32[1024,768]{1,0:T(8,128)S(1)}, ...), condition=%wide.region_23.24_spmd, body=%wide.region_20.23_spmd.sunk | while | flops 2432336384 | bytes 57216936 | solution.py:225
  566.4 34.1 %conditional.5 = ((f32[1024,768]{1,0:T(8,128)S(1)}, f32[3072,3072]{1,0:T(8,128)}, f32[12288,768]{1,0:T(8,128)})) conditional(s32[]{:T(128)} %bitcast.106, (f32[1024,768]{1,0:T(8,128)S(1)}, f32[3072,3072]{1,0:T(8,128)}, f32[12288,768]{1,0:T(8,128)}) %tuple.101, (s32[12]{0:T(128)S(1)}, s32[]{:T(128)}, f32[1024,768]{1,0:T(8,128)S(1)}, ...), branch_computations={%region_21.21_spmd, %region_22.22_spmd} | conditional | flops 2432336384 | bytes 57216656 | solution.py:218
  577.8 9.0 add_dynamic-update-slice_fusion.1
  586.9 9.6 add_dynamic-update-slice_fusion
  601.8 34.1 %conditional.5 = ((f32[1024,768]{1,0:T(8,128)S(1)}, f32[3072,3072]{1,0:T(8,128)}, f32[12288,768]{1,0:T(8,128)})) conditional(s32[]{:T(128)} %bitcast.106, (f32[1024,768]{1,0:T(8,128)S(1)}, f32[3072,3072]{1,0:T(8,128)}, f32[12288,768]{1,0:T(8,128)}) %tuple.101, (s32[12]{0:T(128)S(1)}, s32[]{:T(128)}, f32[1024,768]{1,0:T(8,128)S(1)}, ...), branch_computations={%region_21.21_spmd, %region_22.22_spmd} | conditional | flops 2432336384 | bytes 57216656 | solution.py:218
  613.2 9.0 add_dynamic-update-slice_fusion.1
  622.2 9.6 add_dynamic-update-slice_fusion
  637.2 34.0 %conditional.5 = ((f32[1024,768]{1,0:T(8,128)S(1)}, f32[3072,3072]{1,0:T(8,128)}, f32[12288,768]{1,0:T(8,128)})) conditional(s32[]{:T(128)} %bitcast.106, (f32[1024,768]{1,0:T(8,128)S(1)}, f32[3072,3072]{1,0:T(8,128)}, f32[12288,768]{1,0:T(8,128)}) %tuple.101, (s32[12]{0:T(128)S(1)}, s32[]{:T(128)}, f32[1024,768]{1,0:T(8,128)S(1)}, ...), branch_computations={%region_21.21_spmd, %region_22.22_spmd} | conditional | flops 2432336384 | bytes 57216656 | solution.py:218
  648.5 9.1 add_dynamic-update-slice_fusion.1
  657.6 9.6 add_dynamic-update-slice_fusion
  672.5 34.0 %conditional.5 = ((f32[1024,768]{1,0:T(8,128)S(1)}, f32[3072,3072]{1,0:T(8,128)}, f32[12288,768]{1,0:T(8,128)})) conditional(s32[]{:T(128)} %bitcast.106, (f32[1024,768]{1,0:T(8,128)S(1)}, f32[3072,3072]{1,0:T(8,128)}, f32[12288,768]{1,0:T(8,128)}) %tuple.101, (s32[12]{0:T(128)S(1)}, s32[]{:T(128)}, f32[1024,768]{1,0:T(8,128)S(1)}, ...), branch_computations={%region_21.21_spmd, %region_22.22_spmd} | conditional | flops 2432336384 | bytes 57216656 | solution.py:218
  683.8 9.1 add_dynamic-update-slice_fusion.1
  692.9 9.6 add_dynamic-update-slice_fusion
  707.8 34.2 %conditional.5 = ((f32[1024,768]{1,0:T(8,128)S(1)}, f32[3072,3072]{1,0:T(8,128)}, f32[12288,768]{1,0:T(8,128)})) conditional(s32[]{:T(128)} %bitcast.106, (f32[1024,768]{1,0:T(8,128)S(1)}, f32[3072,3072]{1,0:T(8,128)}, f32[12288,768]{1,0:T(8,128)}) %tuple.101, (s32[12]{0:T(128)S(1)}, s32[]{:T(128)}, f32[1024,768]{1,0:T(8,128)S(1)}, ...), branch_computations={%region_21.21_spmd, %region_22.22_spmd} | conditional | flops 2432336384 | bytes 57216656 | solution.py:218
  719.1 9.2 add_dynamic-update-slice_fusion.1
  728.3 9.7 add_dynamic-update-slice_fusion
  743.3 34.3 %conditional.5 = ((f32[1024,768]{1,0:T(8,128)S(1)}, f32[3072,3072]{1,0:T(8,128)}, f32[12288,768]{1,0:T(8,128)})) conditional(s32[]{:T(128)} %bitcast.106, (f32[1024,768]{1,0:T(8,128)S(1)}, f32[3072,3072]{1,0:T(8,128)}, f32[12288,768]{1,0:T(8,128)}) %tuple.101, (s32[12]{0:T(128)S(1)}, s32[]{:T(128)}, f32[1024,768]{1,0:T(8,128)S(1)}, ...), branch_computations={%region_21.21_spmd, %region_22.22_spmd} | conditional | flops 2432336384 | bytes 57216656 | solution.py:218
  754.6 9.2 add_dynamic-update-slice_fusion.1
  763.8 9.7 add_dynamic-update-slice_fusion
  778.8 34.2 %conditional.5 = ((f32[1024,768]{1,0:T(8,128)S(1)}, f32[3072,3072]{1,0:T(8,128)}, f32[12288,768]{1,0:T(8,128)})) conditional(s32[]{:T(128)} %bitcast.106, (f32[1024,768]{1,0:T(8,128)S(1)}, f32[3072,3072]{1,0:T(8,128)}, f32[12288,768]{1,0:T(8,128)}) %tuple.101, (s32[12]{0:T(128)S(1)}, s32[]{:T(128)}, f32[1024,768]{1,0:T(8,128)S(1)}, ...), branch_computations={%region_21.21_spmd, %region_22.22_spmd} | conditional | flops 2432336384 | bytes 57216656 | solution.py:218
  790.2 9.1 add_dynamic-update-slice_fusion.1
  799.3 9.7 add_dynamic-update-slice_fusion
  814.3 34.0 %conditional.5 = ((f32[1024,768]{1,0:T(8,128)S(1)}, f32[3072,3072]{1,0:T(8,128)}, f32[12288,768]{1,0:T(8,128)})) conditional(s32[]{:T(128)} %bitcast.106, (f32[1024,768]{1,0:T(8,128)S(1)}, f32[3072,3072]{1,0:T(8,128)}, f32[12288,768]{1,0:T(8,128)}) %tuple.101, (s32[12]{0:T(128)S(1)}, s32[]{:T(128)}, f32[1024,768]{1,0:T(8,128)S(1)}, ...), branch_computations={%region_21.21_spmd, %region_22.22_spmd} | conditional | flops 2432336384 | bytes 57216656 | solution.py:218
  825.6 9.1 add_dynamic-update-slice_fusion.1
  834.7 9.5 add_dynamic-update-slice_fusion
  849.5 34.0 %conditional.5 = ((f32[1024,768]{1,0:T(8,128)S(1)}, f32[3072,3072]{1,0:T(8,128)}, f32[12288,768]{1,0:T(8,128)})) conditional(s32[]{:T(128)} %bitcast.106, (f32[1024,768]{1,0:T(8,128)S(1)}, f32[3072,3072]{1,0:T(8,128)}, f32[12288,768]{1,0:T(8,128)}) %tuple.101, (s32[12]{0:T(128)S(1)}, s32[]{:T(128)}, f32[1024,768]{1,0:T(8,128)S(1)}, ...), branch_computations={%region_21.21_spmd, %region_22.22_spmd} | conditional | flops 2432336384 | bytes 57216656 | solution.py:218
  860.9 9.1 add_dynamic-update-slice_fusion.1
  870.0 9.5 add_dynamic-update-slice_fusion
  918.8 8.2 fusion.109
  926.9 8.1 fusion.111
  935.0 36.3 %multiply_reduce_fusion.2 = (f32[4,1024]{1,0:T(4,128)S(1)}, f32[4,1024]{1,0:T(4,128)S(1)}, f32[4,1024]{1,0:T(4,128)S(1)}, f32[4,1024,1024]{1,2,0:T(8,128)}) fusion(f32[4,1024,1024]{1,2,0:T(8,128)} %get-tuple-element.511, f32[4,1024]{1,0:T(4,128)S(1)} %copy-done.25, pred[1024,1024]{0,1:T(8,128)(4,1)S(1)} %copy-done.7, f32[4,1024,1024]{1,2,0:T(8,128)} %fusion.111, ...), kind=kOutput, calls=%fused_computation.74 | convolution fusion | flops 599773184 | bytes 103907328 | tf_op jit(solution)/shard_map/while/body/eval_jaxpr/qhd,khd->hqk/dot_general | solution.py:76
  971.4 42.8 %multiply_convert_fusion.4 = (bf16[4,1024,1024]{1,2,0:T(8,128)(2,1)}, bf16[4,1024,1024]{1,2,0:T(8,128)(2,1)}, bf16[4,1024,1024]{1,2,0:T(8,128)(2,1)}) fusion(f32[4,1024,1024]{1,2,0:T(8,128)} %get-tuple-element.515, f32[4,1024,1024]{1,2,0:T(8,128)} %get-tuple-element.511, f32[4,1024]{1,0:T(4,128)S(1)} %get-tuple-element.435, f32[4,1024]{1,0:T(4,128)S(1)} %copy-done.25, ...), kind=kLoop, calls=%fused_computation.73 | loop fusion | flops 75497472 | bytes 126976000 | tf_op jit(solution)/shard_map/while/body/eval_jaxpr/convert_element_type | solution.py:83
  1033.4 8.0 fusion.94
  1041.4 9.2 fusion.95
  1067.2 8.1 fusion.96
  1086.2 135.2 %psum.7 = s32[4]{0:T(128)} all-reduce(s32[4]{0:T(128)S(1)} %copy-done.54), channel_id=1, replica_groups=mesh['dp'=4,'fsdp'=8] {'dp','fsdp'}, use_global_device_ids=true, to_apply=%region_41.42 | all-reduce | flops 4 | bytes 32 | tf_op jit(solution)/shard_map/psum | solution.py:275
  1221.4 9.2 fusion.138
  1249.3 42.8 %all-reduce.2 = (f32[768,2]{0,1:T(2,128)S(1)}, f32[768,2]{0,1:T(2,128)S(1)}) all-reduce(f32[768,2]{0,1:T(2,128)S(1)} %pad_maximum_fusion.2, f32[768,2]{0,1:T(2,128)S(1)} %pad_maximum_fusion.3), channel_id=4, replica_groups=mesh['dp'=4,'fsdp'=8] {'dp','fsdp'}, use_global_device_ids=true, to_apply=%region_35.36.clone | all-reduce | flops 3072 | bytes 24576
  1293.3 86.4 %reduce-scatter.7.cloned.1.call-done = f32[24,2304]{1,0:T(8,128)} async-done(((f32[768,2304]{1,0:T(8,128)}), f32[24,2304]{1,0:T(8,128)}) %reduce-scatter.7.cloned.1.call-update) | async-done | bytes 221200 | tf_op jit(solution)/shard_map/reduce_scatter | solution.py:334
  1379.7 354.5 %reduce-scatter.11.cloned.1.call-done = f32[96,3072]{1,0:T(8,128)} async-done(((f32[3072,3072]{1,0:T(8,128)}), f32[96,3072]{1,0:T(8,128)}) %reduce-scatter.11.cloned.1.call-update) | async-done | bytes 1179664 | tf_op jit(solution)/shard_map/reduce_scatter | solution.py:301
  1734.3 355.8 %reduce-scatter.13.cloned.1.call-done = f32[384,768]{1,0:T(8,128)} async-done(((f32[12288,768]{1,0:T(8,128)}), f32[384,768]{1,0:T(8,128)}) %reduce-scatter.13.cloned.1.call-update) | async-done | bytes 1179664 | tf_op jit(solution)/shard_map/reduce_scatter | solution.py:302
  (403 shorter events, 415.7 us)
Async XLA Ops:
  7.2 85.5 %copy-start = (s32[8008]{0:T(1024)S(1)}, s32[8008]{0:T(1024)}, u32[]{:S(2)}) copy-start(s32[8008]{0:T(1024)} %param.26) | copy-start | bytes 96100
  7.2 4.7 copy-start.51
  7.2 48.1 %copy-start.52 = (bf16[24,2]{0,1:T(2,128)(2,1)S(1)}, bf16[24,2]{0,1:T(2,128)(2,1)}, u32[]{:S(2)}) copy-start(bf16[24,2]{0,1:T(2,128)(2,1)} %param.30) | copy-start | bytes 292
  7.2 85.4 %copy-start.50 = (s32[1024]{0:T(1024)S(1)}, s32[1024]{0:T(1024)}, u32[]{:S(2)}) copy-start(s32[1024]{0:T(1024)} %param.24) | copy-start | bytes 12292
  7.2 111.1 %all-gather.7.cloned.1.call-start = ((), (), s32[]{:S(2)}) async-start(), calls=%async_computation.4 | async-start | bytes 3649536 | tf_op jit(solution)/shard_map/all_gather | solution.py:248
  8.0 211.4 %all-gather.9.cloned.1.call-start = ((), (), s32[]{:S(2)}) async-start(), calls=%async_computation.5 | async-start | bytes 1216512 | tf_op jit(solution)/shard_map/all_gather | solution.py:249
  8.7 249.3 %all-gather.11.cloned.1.call-start = ((), (), s32[]{:S(2)}) async-start(), calls=%async_computation.6 | async-start | bytes 19464192 | tf_op jit(solution)/shard_map/all_gather | solution.py:285
  9.4 374.2 %all-gather.13.cloned.1.call-start = ((), (), s32[]{:S(2)}) async-start(), calls=%async_computation.7 | async-start | bytes 19464192 | tf_op jit(solution)/shard_map/all_gather | solution.py:286
  10.0 1283.3 %reduce-scatter.9.cloned.1.call-start = ((), (), s32[]{:S(2)}) async-start(), calls=%async_computation.9 | async-start | bytes 2433024 | tf_op jit(solution)/shard_map/reduce_scatter | solution.py:335
  10.1 94.9 %copy-start.4 = (bf16[1024,768]{1,0:T(8,128)(2,1)S(1)}, bf16[1024,768]{1,0:T(8,128)(2,1)}, u32[]{:S(2)}) copy-start(bf16[1024,768]{1,0:T(8,128)(2,1)} %param.33) | copy-start | bytes 4718596
  11.9 207.6 %copy-start.10 = (bf16[1024,768]{0,1:T(8,128)(2,1)}, bf16[1024,768]{0,1:T(8,128)(2,1)S(1)}, u32[]{:S(2)}) copy-start(bf16[1024,768]{0,1:T(8,128)(2,1)S(1)} %copy.120) | copy-start | bytes 4718596
  103.3 3.2 copy-start.53
  116.4 10.1 copy-start.42
  116.5 10.1 copy-start.48
  116.5 106.7 %copy-start.38 = (f32[768]{0:T(1024)}, f32[768]{0:T(1024)S(1)}, u32[]{:S(2)}) copy-start(f32[768]{0:T(1024)S(1)} %get-tuple-element.519) | copy-start | bytes 9220
  116.9 9.6 copy-start.36
  117.4 9.1 copy-start.44
  118.3 90.7 %copy-start.6 = (pred[1024,1024]{0,1:T(8,128)(4,1)}, pred[1024,1024]{0,1:T(8,128)(4,1)S(1)}, u32[]{:S(2)}) copy-start(pred[1024,1024]{0,1:T(8,128)(4,1)S(1)} %fusion.70) | copy-start | bytes 3145732
  133.2 3.5 copy-start.12
  136.7 8.5 copy-start.19
  172.9 13.5 copy-start.24
  186.4 10.1 copy-start.26
  186.4 22.6 %copy-start.22 = (f32[4,1024]{1,0:T(4,128)}, f32[4,1024]{1,0:T(4,128)S(1)}, u32[]{:S(2)}) copy-start(f32[4,1024]{1,0:T(4,128)S(1)} %log_add_fusion) | copy-start | bytes 49156
  219.3 3.4 copy-start.20
  539.4 13.0 copy-start.2
  565.0 322.4 %copy-start.46 = (s32[1024]{0:T(1024)S(1)}, s32[1024]{0:T(1024)}, u32[]{:S(2)}) copy-start(s32[1024]{0:T(1024)} %fusion.120) | copy-start | bytes 12292
  586.8 9.7 copy-start.5
  622.2 9.7 copy-start.5
  657.6 9.6 copy-start.5
  692.9 9.6 copy-start.5
  728.3 9.7 copy-start.5
  763.8 9.7 copy-start.5
  799.3 9.7 copy-start.5
  834.7 9.5 copy-start.5
  870.0 9.5 copy-start.5
  892.6 3.6 copy-start.35
  892.6 3.6 copy-start.39
  892.6 3.6 copy-start.41
  896.2 4.6 copy-start.3
  906.1 4.1 copy-start.9
  910.1 6.1 copy-start.55
  926.9 8.1 copy-start.7
  926.9 8.1 copy-start.23
  926.9 8.1 copy-start.25
  926.9 8.1 copy-start.27
  1014.1 13.3 slice-start
  1014.1 13.3 slice-start.2
  1020.2 7.2 slice-start.1
  1020.2 7.2 slice-start.3
  1041.4 9.2 copy-start.15
  1041.4 9.2 copy-start.21
  1059.4 320.3 %reduce-scatter.7.cloned.1.call-start = ((), (), s32[]{:S(2)}) async-start(), calls=%async_computation.8 | async-start | bytes 7299072 | tf_op jit(solution)/shard_map/reduce_scatter | solution.py:334
  1059.5 6.4 copy-start.31
  1059.5 6.3 copy-start.32
  1059.5 6.3 copy-start.33
  1067.2 8.1 copy-start.28
  1075.5 2.8 copy-start.11
  1075.5 2.8 copy-start.37
  1084.7 649.5 %reduce-scatter.11.cloned.1.call-start = ((), (), s32[]{:S(2)}) async-start(), calls=%async_computation.10 | async-start | bytes 38928384 | tf_op jit(solution)/shard_map/reduce_scatter | solution.py:301
  1085.5 1004.5 %reduce-scatter.13.cloned.1.call-start = ((), (), s32[]{:S(2)}) async-start(), calls=%async_computation.11 | async-start | bytes 38928384 | tf_op jit(solution)/shard_map/reduce_scatter | solution.py:302
  1236.3 3.1 copy-start.47
  1236.3 3.1 copy-start.13
  1244.0 3.7 copy-start.16
  1244.0 846.0 %copy-start.1 = (s32[8008]{0:T(1024)S(1)}, s32[8008]{0:T(1024)}, u32[]{:S(2)}) copy-start(s32[8008]{0:T(1024)} %param.26) | copy-start | bytes 96100
  (12 other events, 23.8 us)
Sparse Core Ops, SparseCore 0:
  11.0 62.8 all-gather.6
  76.8 54.5 all-gather.8
  134.3 123.6 all-gather.10
  260.7 122.8 all-gather.12
  1059.5 194.9 reduce-scatter.8
  1261.5 118.1 reduce-scatter.6
  1386.7 347.4 reduce-scatter.10
  1742.4 347.5 reduce-scatter.12
where the time goes:
time: 2100 us
  waiting for transfers between devices  953 us (45%)
  matrix products  548 us (26%)
  blocking collectives  257 us (12%)
  local copies, waits for them, and re-layouts  160 us (8%)
  other arithmetic  110 us (5%)
  loops' own time  52.3 us (2%)
    reduce_scatter x1, waiting for transfers between devices, body(): lax.psum_scatter(grad_outer, ('dp', 'fsdp'), scatter_dimension=0, tiled=T...  356 us
    reduce_scatter x1, waiting for transfers between devices, body(): lax.psum_scatter(grad_inner, ('dp', 'fsdp'), scatter_dimension=0, tiled=T...  355 us
    psum x1, blocking collectives, body(): expert_counts = lax.psum(local_counts, ('dp', 'fsdp'))  135 us
    all_gather x1, waiting for transfers between devices, body(): lax.all_gather(w_out, ('dp', 'fsdp'), axis=0, tiled=True)  126 us
    dot_general x9, matrix products, compute(): jnp.einsum('tf,td->fd', activated.astype(jnp.bfloat16), grad_block, prefe...  86.5 us
    reduce_scatter x1, waiting for transfers between devices, body(): lax.psum_scatter(grad_qkv_w, ('dp', 'fsdp'), scatter_dimension=0, tiled=T...  86.4 us
    dot_general x9, matrix products, compute(): jnp.einsum('td,tf->df', rows_here, grad_pre, preferred_element_type=jnp.f...  81.9 us
    dynamic_slice x96, local copies, waits for them, and re-layouts, expert_forward(): final_state, _ = lax.scan(visit, start_state, table)  57.9 us
  transfers between devices with their start and end apart: 8, of which 5 were waited for; matrix products, arithmetic and copies ran while one was open for 9% of the time, Pallas kernels for 0%

commit v1 on v0

--- a/solution.py
+++ b/solution.py
@@ -1,6 +1,8 @@
 import jax
 import jax.numpy as jnp
 from jax import lax
+from jax.experimental import pallas as pl
+from jax.experimental.pallas import tpu as pltpu
 from jax.sharding import PartitionSpec as P
 
 D = 768
@@ -349,6 +351,579 @@
     )
 
 
+LOG2E = 1.4426950408889634
+ROWS = 256
+GROUP = 16
+MIB = 1024 * 1024
+NT = (((1,), (1,)), ((), ()))
+NN = (((1,), (0,)), ((), ()))
+ROOT = 0.7978845608028654
+CUBIC = 0.044715
+
+
+def mul(a, b, dims=NN):
+    return lax.dot_general(a, b, dims, preferred_element_type=jnp.float32)
+
+
+def iota(shape, dim):
+    return lax.broadcasted_iota(jnp.int32, shape, dim)
+
+
+def padded_rows(slots):
+    return slots + EXPERTS * GROUP
+
+
+def three_parts(v):
+    first = v.astype(jnp.bfloat16)
+    rest = v - first.astype(jnp.float32)
+    second = rest.astype(jnp.bfloat16)
+    third = (rest - second.astype(jnp.float32)).astype(jnp.bfloat16)
+    return first, second, third
+
+
+def own_lanes(lane, half):
+    return (lane < HEAD_DIM) if half == 0 else (lane >= HEAD_DIM)
+
+
+def extra_lane(half):
+    return HEAD_DIM if half == 0 else 0
+
+
+def routing(ids, table, length, perm_ref):
+    slots = ids.shape[1]
+    chosen = (iota((table.shape[1], slots), 0) == (ids >> 7)).astype(jnp.bfloat16)
+    rows = mul(table, chosen)
+    expert = jnp.sum(
+        jnp.where(iota(rows.shape, 0) == (ids & 127), rows, 0.0), axis=0, keepdims=True
+    ).astype(jnp.int32)
+    used = iota((1, slots), 1) < length
+    member = (iota((8, slots), 0) == expert) & used
+    member_f = jnp.where(member, 1.0, 0.0)
+    perm_ref[0:slots, :] = (iota((slots, slots), 0) <= iota((slots, slots), 1)).astype(jnp.bfloat16)
+    rank = mul(member_f.astype(jnp.bfloat16), perm_ref[0:slots, :])
+    counts = rank[:, slots - 1 : slots]
+    groups = jnp.floor((counts + (GROUP - 1)) * (1.0 / GROUP))
+    row8 = iota((8, 1), 0)
+    start = jnp.zeros((8, 1), jnp.float32)
+    for e in range(EXPERTS - 1):
+        start = start + jnp.where(row8 > e, groups[e : e + 1, :], 0.0)
+    place = jnp.sum(member_f * (rank - 1.0 + start * GROUP), axis=0, keepdims=True)
+    place = jnp.where(used, place, -1.0)
+    return place, counts, groups
+
+
+def front_kernel(
+    len_ref, x_ref, ids_ref, table_ref, g_ref, wa_ref, norms_ref,
+    qkv_ref, mixed_ref, aug_ref, hidden_ref, xs_ref, gs_ref, pos_ref, counts_ref,
+    perm_ref, normed_ref, qa_ref, ka_ref, va_ref,
+):
+    slots, width = x_ref.shape
+    heads = width // HEAD_DIM
+    rp = padded_rows(slots)
+    length = len_ref[0]
+
+    place, counts, groups = routing(ids_ref[...], table_ref[...], length, perm_ref)
+    pos_ref[...] = jnp.broadcast_to(place, (128, slots)).T
+    counts_ref[...] = jnp.broadcast_to(counts, (8, 128)).astype(jnp.int32)
+    place_i = place.astype(jnp.int32)
+    step = rp // 4
+
+    @pl.loop(0, 4)
+    def _(i):
+        base = i * step
+        perm_ref[pl.ds(base, step), :] = (
+            iota((step, slots), 0) + base == place_i
+        ).astype(jnp.bfloat16)
+        gs_ref[pl.ds(base, step), :] = mul(perm_ref[pl.ds(base, step), :], g_ref[...]).astype(jnp.bfloat16)
+
+    tail = jnp.broadcast_to(jnp.concatenate([groups, groups], axis=0), (GROUP, width)).astype(jnp.bfloat16)
+    xs_ref[rp : rp + GROUP, :] = tail
+    gs_ref[rp : rp + GROUP, :] = tail
+
+    @pl.loop(0, slots // ROWS)
+    def _(i):
+        rows = pl.ds(i * ROWS, ROWS)
+        normal, _ = layer_stats(x_ref[rows, :].astype(jnp.float32))
+        normed = (normal * norms_ref[0:1, :] + norms_ref[2:3, :]).astype(jnp.bfloat16)
+        for c in range(3):
+            cols = slice(c * width, (c + 1) * width)
+            qkv_ref[rows, cols] = mul(normed, wa_ref[:, cols]).astype(jnp.bfloat16)
+
+    lane = iota((slots, 128), 1)
+    key_bias = jnp.where(iota((slots, 128), 0) < length, 0.0, NEGATIVE).astype(jnp.bfloat16)
+    causal = iota((ROWS, ROWS), 1) <= iota((ROWS, ROWS), 0)
+    lane_b = iota((ROWS, 128), 1)
+
+    @pl.loop(0, heads // 2)
+    def _(p):
+        cols = pl.ds(p * 128, 128)
+        q = qkv_ref[:, cols].astype(jnp.float32) * (HEAD_DIM ** -0.5 * LOG2E)
+        q_hi = q.astype(jnp.bfloat16)
+        q_lo = (q - q_hi.astype(jnp.float32)).astype(jnp.bfloat16)
+        k = qkv_ref[:, pl.ds(width + p * 128, 128)]
+        v = qkv_ref[:, pl.ds(2 * width + p * 128, 128)]
+        zero = jnp.zeros_like(q_hi)
+        one = jnp.ones_like(q_hi)
+        sides = []
+        for half in range(2):
+            own = own_lanes(lane, half)
+            extra = extra_lane(half)
+            qa_ref[half, :, 0:128] = jnp.where(own, q_hi, zero)
+            qa_ref[half, :, 128:256] = jnp.where(own, q_lo, jnp.where(lane == extra, one, zero))
+            ka_ref[half, :, 0:128] = k
+            ka_ref[half, :, 128:256] = jnp.where(own, k, jnp.where(lane == extra, key_bias, zero))
+            va_ref[half, :, :] = jnp.where(own, v, one)
+        for i in range(slots // ROWS):
+            rows = slice(i * ROWS, (i + 1) * ROWS)
+            keys = (i + 1) * ROWS
+            outs = []
+            for half in range(2):
+                s = mul(qa_ref[half, rows, :], ka_ref[half, 0:keys, :], NT)
+                diag = jnp.where(causal, s[:, i * ROWS :], NEGATIVE)
+                s = diag if i == 0 else jnp.concatenate([s[:, : i * ROWS], diag], axis=1)
+                top = jnp.max(s, axis=1, keepdims=True)
+                probs = jnp.exp2(s - top).astype(jnp.bfloat16)
+                out = mul(probs, va_ref[half, 0:keys, :])
+                total = pltpu.roll(out, HEAD_DIM, 1)
+                outs.append(out / total)
+                minus = -(top + jnp.log2(out))
+                a, b, c = three_parts(minus)
+                extra = extra_lane(half)
+                seen = qa_ref[half, rows, 128:256]
+                seen = jnp.where(lane_b == extra + 1, a, seen)
+                seen = jnp.where(lane_b == extra + 2, b, seen)
+                seen = jnp.where(lane_b == extra + 3, c, seen)
+                aug_ref[2 * p + half, rows, :] = seen
+            mixed_ref[rows, cols] = jnp.where(lane_b < HEAD_DIM, outs[0], outs[1]).astype(jnp.bfloat16)
+
+    @pl.loop(0, slots // ROWS)
+    def _(i):
+        rows = pl.ds(i * ROWS, ROWS)
+        hidden = x_ref[rows, :].astype(jnp.float32) + mul(mixed_ref[rows, :], wa_ref[:, 3 * width :])
+        hidden_ref[rows, :] = hidden
+        normal, _ = layer_stats(hidden)
+        normed_ref[rows, :] = (normal * norms_ref[1:2, :] + norms_ref[3:4, :]).astype(jnp.bfloat16)
+
+    @pl.loop(0, 4)
+    def _(i):
+        rows = pl.ds(i * step, step)
+        xs_ref[rows, :] = mul(perm_ref[rows, :], normed_ref[...]).astype(jnp.bfloat16)
+
+
+def front(length, x, ids, table, g, wa, norms):
+    slots, width = x.shape
+    rp = padded_rows(slots)
+    bf = jnp.bfloat16
+    whole = pl.BlockSpec(memory_space=pltpu.VMEM)
+    return pl.pallas_call(
+        front_kernel,
+        out_shape=(
+            jax.ShapeDtypeStruct((slots, 3 * width), bf),
+            jax.ShapeDtypeStruct((slots, width), bf),
+            jax.ShapeDtypeStruct((HEADS, slots, 128), bf),
+            jax.ShapeDtypeStruct((slots, width), jnp.float32),
+            jax.ShapeDtypeStruct((rp + GROUP, width), bf),
+            jax.ShapeDtypeStruct((rp + GROUP, width), bf),
+            jax.ShapeDtypeStruct((slots, 128), jnp.float32),
+            jax.ShapeDtypeStruct((8, 128), jnp.int32),
+        ),
+        in_specs=[pl.BlockSpec(memory_space=pltpu.SMEM)] + [whole] * 6,
+        out_specs=tuple([whole] * 8),
+        scratch_shapes=[
+            pltpu.VMEM((rp, slots), bf),
+            pltpu.VMEM((slots, width), bf),
+            pltpu.VMEM((2, slots, 256), bf),
+            pltpu.VMEM((2, slots, 256), bf),
+            pltpu.VMEM((2, slots, 128), bf),
+        ],
+        compiler_params=pltpu.CompilerParams(vmem_limit_bytes=56 * MIB),
+        name="front",
+    )(length, x, ids, table, g, wa, norms)
+
+
+CHUNK = 32
+
+
+def experts_kernel(
+    n_ref, x_ref, g_ref, w1_ref, w2_ref,
+    o_ref, dx_ref, gw1_ref, gw2_ref,
+    xb, gb, ob, db, acc1, acc2, blank, sem_in, sem_out, sem_zero,
+):
+    sources, groups, _, width = x_ref.shape
+    groups = groups - 1
+    hidden = w2_ref.shape[1]
+    rows = CHUNK * GROUP
+
+    blank[...] = jnp.zeros_like(blank)
+    xb[...] = jnp.zeros_like(xb)
+    gw1_ref[...] = jnp.zeros_like(gw1_ref)
+    gw2_ref[...] = jnp.zeros_like(gw2_ref)
+
+    totals = []
+    for e in range(EXPERTS):
+        totals.append(lax.fori_loop(0, sources, lambda s, t, e=e: t + n_ref[s * EXPERTS + e], 0))
+    first = [0]
+    for e in range(EXPERTS):
+        first.append(first[-1] + (totals[e] + (CHUNK - 1)) // CHUNK)
+    chunks = first[EXPERTS]
+
+    def pick(values, e):
+        out = values[0]
+        for i in range(1, EXPERTS):
+            out = jnp.where(e == i, values[i], out)
+        return out
+
+    def locate(c):
+        e = jnp.int32(0)
+        for i in range(1, EXPERTS):
+            e = e + jnp.where(c >= first[i], 1, 0)
+        begin = (c - pick(first, e)) * CHUNK
+        return e, begin, jnp.minimum(begin + CHUNK, pick(totals, e))
+
+    def pieces(c, act):
+        e, begin, end = locate(c)
+
+        def visit(s, base):
+            n = n_ref[s * EXPERTS + e]
+            low = jnp.maximum(base, begin)
+            size = jnp.minimum(base + n, end) - low
+            skip = jnp.int32(0)
+            for i in range(EXPERTS - 1):
+                skip = skip + jnp.where(e > i, n_ref[s * EXPERTS + i], 0)
+
+            @pl.when(size > 0)
+            def _():
+                act(s, skip + low - base, low - begin, size)
+
+            return base + n
+
+        lax.fori_loop(0, sources, visit, jnp.int32(0))
+
+    def load(c, slot):
+        def act(s, at, to, size):
+            for k, (src, dst) in enumerate(((x_ref, xb), (g_ref, gb))):
+                pltpu.make_async_copy(
+                    src.at[s, pl.ds(at, size)], dst.at[slot, pl.ds(to, size)], sem_in.at[k, slot]
+                ).start()
+
+        pieces(c, act)
+
+    def store(c, slot):
+        def act(s, at, to, size):
+            for k, (src, dst) in enumerate(((ob, o_ref), (db, dx_ref))):
+                pltpu.make_async_copy(
+                    src.at[slot, pl.ds(to, size)], dst.at[s, pl.ds(at, size)], sem_out.at[k, slot]
+                ).start()
+
+        pieces(c, act)
+
+    def settle(c, slot, bufs, sems):
+        _, begin, end = locate(c)
+        for k, buf in enumerate(bufs):
+            part = buf.at[slot, pl.ds(0, end - begin)]
+            pltpu.make_async_copy(part, part, sems.at[k, slot]).wait()
+
+    def used_groups(s):
+        t = n_ref[s * EXPERTS]
+        for e in range(1, EXPERTS):
+            t = t + n_ref[s * EXPERTS + e]
+        return t
+
+    def rest(s, act):
+        t = used_groups(s)
+
+        @pl.when(groups - t > 0)
+        def _():
+            for k, dst in enumerate((o_ref, dx_ref)):
+                act(
+                    pltpu.make_async_copy(
+                        blank.at[pl.ds(0, groups - t)], dst.at[s, pl.ds(t, groups - t)], sem_zero.at[k, s]
+                    )
+                )
+
+    @pl.loop(0, sources)
+    def _(s):
+        rest(s, lambda copy: copy.start())
+
+    @pl.when(chunks > 0)
+    def _():
+        load(0, 0)
+
+    @pl.loop(0, chunks)
+    def _(c):
+        slot = c % 2
+        e, begin, end = locate(c)
+
+        @pl.when(c + 1 < chunks)
+        def _():
+            load(c + 1, 1 - slot)
+
+        settle(c, slot, (xb, gb), sem_in)
+
+        @pl.when(c >= 2)
+        def _():
+            settle(c - 2, slot, (ob, db), sem_out)
+
+        x = xb[slot].reshape(rows, width)
+        g = gb[slot].reshape(rows, width)
+        g = jnp.where(iota((rows, width), 0) < (end - begin) * GROUP, g, jnp.zeros_like(g))
+        w1 = w1_ref[e]
+        w2 = w2_ref[e]
+        pre = mul(x, w1)
+        square = pre * pre
+        t = jnp.tanh(ROOT * pre * (1.0 + CUBIC * square))
+        act = (0.5 * pre * (1.0 + t)).astype(jnp.bfloat16)
+        slope = 0.5 * (1.0 + t) + 0.5 * pre * (1.0 - t * t) * (ROOT * (1.0 + 3.0 * CUBIC * square))
+        grad_pre = (slope * mul(g, w2, NT)).astype(jnp.bfloat16)
+        ob[slot] = mul(act, w2).astype(jnp.bfloat16).reshape(CHUNK, GROUP, width)
+        db[slot] = mul(grad_pre, w1, NT).astype(jnp.bfloat16).reshape(CHUNK, GROUP, width)
+        store(c, slot)
+        add1 = mul(grad_pre.T, x)
+        add2 = mul(act.T, g)
+
+        @pl.when(begin == 0)
+        def _():
+            acc1[...] = add1
+            acc2[...] = add2
+
+        @pl.when(begin > 0)
+        def _():
+            acc1[...] += add1
+            acc2[...] += add2
+
+        @pl.when(end == pick(totals, e))
+        def _():
+            gw1_ref[e] = acc1[...].astype(gw1_ref.dtype)
+            gw2_ref[e] = acc2[...].astype(gw2_ref.dtype)
+
+    @pl.when(chunks >= 2)
+    def _():
+        settle(chunks - 2, chunks % 2, (ob, db), sem_out)
+
+    @pl.when(chunks >= 1)
+    def _():
+        settle(chunks - 1, (chunks - 1) % 2, (ob, db), sem_out)
+
+    @pl.loop(0, sources)
+    def _(s):
+        rest(s, lambda copy: copy.wait())
+
+
+def experts(n16, xs, gs, w1, w2):
+    sources, groups, _, width = xs.shape
+    hidden = w2.shape[1]
+    bf = jnp.bfloat16
+    whole = pl.BlockSpec(memory_space=pltpu.VMEM)
+    far = pl.BlockSpec(memory_space=pl.ANY)
+    out_rows = jax.ShapeDtypeStruct((sources, groups - 1, GROUP, width), bf)
+    return pl.pallas_call(
+        experts_kernel,
+        out_shape=(
+            out_rows, out_rows,
+            jax.ShapeDtypeStruct((EXPERTS, hidden, width), bf),
+            jax.ShapeDtypeStruct((EXPERTS, hidden, width), bf),
+        ),
+        in_specs=[pl.BlockSpec(memory_space=pltpu.SMEM), far, far, whole, whole],
+        out_specs=(far, far, whole, whole),
+        scratch_shapes=[pltpu.VMEM((2, CHUNK, GROUP, width), bf)] * 4
+        + [pltpu.VMEM((hidden, width), jnp.float32)] * 2
+        + [pltpu.VMEM((groups - 1, GROUP, width), bf)]
+        + [pltpu.SemaphoreType.DMA((2, 2)), pltpu.SemaphoreType.DMA((2, 2)), pltpu.SemaphoreType.DMA((2, sources))],
+        compiler_params=pltpu.CompilerParams(vmem_limit_bytes=56 * MIB),
+        name="experts",
+    )(n16, xs, gs, w1, w2)
+
+
+def back_kernel(
+    len_ref, x_ref, g_ref, hidden_ref, qkv_ref, mixed_ref, aug_ref, pos_ref, dxs_ref, os_ref, wa_ref, norms_ref,
+    out_ref, gx_ref, gwa_ref, gn_ref,
+    branch_ref, gmix_ref, gqkv_ref, tr_ref, qa_ref, ka_ref, va_ref, oa_ref, dv_ref, dk_ref, dq_ref,
+):
+    slots, width = x_ref.shape
+    heads = width // HEAD_DIM
+    rp = dxs_ref.shape[0]
+    length = len_ref[0]
+    scale = HEAD_DIM ** -0.5
+    gn_ref[...] = jnp.zeros_like(gn_ref)
+
+    @pl.loop(0, slots // ROWS)
+    def _(i):
+        rows = pl.ds(i * ROWS, ROWS)
+        place = pos_ref[rows, 0:1].astype(jnp.int32)
+        pick = (iota((ROWS, rp), 1) == place).astype(jnp.bfloat16)
+        hidden = hidden_ref[rows, :]
+        out_ref[rows, :] = (hidden + mul(pick, os_ref[...])).astype(jnp.bfloat16)
+        grad = mul(pick, dxs_ref[...])
+        normal, scaled = layer_stats(hidden)
+        gn_ref[1:2, :] += jnp.sum(grad * normal, axis=0, keepdims=True)
+        gn_ref[3:4, :] += jnp.sum(grad, axis=0, keepdims=True)
+        grad_hidden = g_ref[rows, :].astype(jnp.float32) + norm_backward(grad, normal, scaled, norms_ref[1:2, :])
+        gx_ref[rows, :] = grad_hidden
+        branch = grad_hidden.astype(jnp.bfloat16)
+        branch_ref[rows, :] = branch
+        gmix_ref[rows, :] = mul(branch, wa_ref[:, 3 * width :], NT).astype(jnp.bfloat16)
+
+    tr_ref[...] = mixed_ref[...].T
+    tile = width // 3
+
+    @pl.loop(0, 3)
+    def _(i):
+        rows = pl.ds(i * tile, tile)
+        gwa_ref[rows, 3 * width :] = mul(tr_ref[rows, :], branch_ref[...]).astype(gwa_ref.dtype)
+
+    lane = iota((slots, 128), 1)
+    key_bias = jnp.where(iota((slots, 128), 0) < length, 0.0, NEGATIVE).astype(jnp.bfloat16)
+    causal = iota((ROWS, ROWS), 0) <= iota((ROWS, ROWS), 1)
+
+    @pl.loop(0, heads // 2)
+    def _(p):
+        cols = pl.ds(p * 128, 128)
+        q = qkv_ref[:, cols]
+        q_hi = (q.astype(jnp.float32) * (scale * LOG2E)).astype(jnp.bfloat16)
+        k = qkv_ref[:, pl.ds(width + p * 128, 128)]
+        v = qkv_ref[:, pl.ds(2 * width + p * 128, 128)]
+        do = gmix_ref[:, cols]
+        prod = do.astype(jnp.float32) * mixed_ref[:, cols].astype(jnp.float32)
+        k_t = k.T
+        zero = jnp.zeros_like(q)
+        one = jnp.ones_like(q)
+        for half in range(2):
+            own = own_lanes(lane, half)
+            extra = extra_lane(half)
+            parts = (lane > extra) & (lane <= extra + 3)
+            qa_ref[half, :, 0:128] = jnp.where(own, q_hi, zero)
+            qa_ref[half, :, 128:256] = aug_ref[2 * p + half]
+            ka_ref[half, :, 0:128] = k
+            ka_ref[half, :, 128:256] = jnp.where(
+                own, k, jnp.where(lane == extra, key_bias, jnp.where(parts, one, zero))
+            )
+            va_ref[half, :, :] = jnp.where(own, v, jnp.where(parts, one, zero))
+            minus = -jnp.sum(jnp.where(own, prod, 0.0), axis=1, keepdims=True)
+            a, b, c = three_parts(jnp.broadcast_to(minus, (slots, 128)))
+            oa_ref[half, :, :] = jnp.where(
+                own, do,
+                jnp.where(lane == extra + 1, a, jnp.where(lane == extra + 2, b, jnp.where(lane == extra + 3, c, zero))),
+            )
+        for half in range(2):
+            k_own = k_t[half * HEAD_DIM : (half + 1) * HEAD_DIM, :]
+            heads_rows = slice(half * HEAD_DIM, (half + 1) * HEAD_DIM)
+            for j in range(slots // ROWS):
+                keys = slice(j * ROWS, (j + 1) * ROWS)
+                late = slice(j * ROWS, slots)
+                s = mul(ka_ref[half, keys, :], qa_ref[half, late, :], NT)
+                diag = jnp.where(causal, s[:, :ROWS], NEGATIVE)
+                s = diag if j == slots // ROWS - 1 else jnp.concatenate([diag, s[:, ROWS:]], axis=1)
+                probs = jnp.exp2(s)
+                dp = mul(va_ref[half, keys, :], oa_ref[half, late, :], NT)
+                ds = (probs * dp).astype(jnp.bfloat16)
+                probs = probs.astype(jnp.bfloat16)
+                dv_ref[half, keys, :] = mul(probs, gmix_ref[late, cols])
+                dk_ref[half, keys, :] = mul(ds, qkv_ref[late, cols])
+                dq = mul(k_own[:, keys], ds)
+                if j == 0:
+                    dq_ref[heads_rows, late] = dq
+                else:
+                    dq_ref[heads_rows, late] += dq
+        first = lane < HEAD_DIM
+        gqkv_ref[:, cols] = (dq_ref[...].T * scale).astype(jnp.bfloat16)
+        gqkv_ref[:, pl.ds(width + p * 128, 128)] = (jnp.where(first, dk_ref[0], dk_ref[1]) * scale).astype(jnp.bfloat16)
+        gqkv_ref[:, pl.ds(2 * width + p * 128, 128)] = jnp.where(first, dv_ref[0], dv_ref[1]).astype(jnp.bfloat16)
+
+    @pl.loop(0, slots // ROWS)
+    def _(i):
+        rows = pl.ds(i * ROWS, ROWS)
+        normal, scaled = layer_stats(x_ref[rows, :].astype(jnp.float32))
+        branch_ref[rows, :] = (normal * norms_ref[0:1, :] + norms_ref[2:3, :]).astype(jnp.bfloat16)
+        grad = mul(gqkv_ref[rows, :], wa_ref[:, : 3 * width], NT)
+        gn_ref[0:1, :] += jnp.sum(grad * normal, axis=0, keepdims=True)
+        gn_ref[2:3, :] += jnp.sum(grad, axis=0, keepdims=True)
+        gx_ref[rows, :] += norm_backward(grad, normal, scaled, norms_ref[0:1, :])
+
+    tr_ref[...] = branch_ref[...].T
+
+    @pl.loop(0, 3)
+    def _(i):
+        rows = pl.ds(i * tile, tile)
+        for c in range(3):
+            cols = slice(c * width, (c + 1) * width)
+            gwa_ref[rows, cols] = mul(tr_ref[rows, :], gqkv_ref[:, cols]).astype(gwa_ref.dtype)
+
+
+def back(length, x, g, hidden, qkv, mixed, aug, pos, dxs, os, wa, norms):
+    slots, width = x.shape
+    bf = jnp.bfloat16
+    f32 = jnp.float32
+    whole = pl.BlockSpec(memory_space=pltpu.VMEM)
+    return pl.pallas_call(
+        back_kernel,
+        out_shape=(
+            jax.ShapeDtypeStruct((slots, width), bf),
+            jax.ShapeDtypeStruct((slots, width), f32),
+            jax.ShapeDtypeStruct((width, 4 * width), bf),
+            jax.ShapeDtypeStruct((8, width), f32),
+        ),
+        in_specs=[pl.BlockSpec(memory_space=pltpu.SMEM)] + [whole] * 11,
+        out_specs=tuple([whole] * 4),
+        scratch_shapes=[
+            pltpu.VMEM((slots, width), bf),
+            pltpu.VMEM((slots, width), bf),
+            pltpu.VMEM((slots, 3 * width), bf),
+            pltpu.VMEM((width, slots), bf),
+            pltpu.VMEM((2, slots, 256), bf),
+            pltpu.VMEM((2, slots, 256), bf),
+            pltpu.VMEM((2, slots, 128), bf),
+            pltpu.VMEM((2, slots, 128), bf),
+            pltpu.VMEM((2, slots, 128), f32),
+            pltpu.VMEM((2, slots, 128), f32),
+            pltpu.VMEM((128, slots), f32),
+        ],
+        compiler_params=pltpu.CompilerParams(vmem_limit_bytes=60 * MIB),
+        name="back",
+    )(length, x, g, hidden, qkv, mixed, aug, pos, dxs, os, wa, norms)
+
+
+def plane_body(
+    tokens, token_ids, lengths, hash_table, w_qkv, w_attn_out, norm_gains, norm_biases, w_in, w_out, cotangent
+):
+    slots, width = tokens.shape
+    bf = jnp.bfloat16
+    both = ("dp", "fsdp")
+    plane = lax.axis_size("fsdp")
+    part = w_in.shape[1] // plane
+    rp = padded_rows(slots)
+
+    norm_cols = jnp.concatenate([norm_gains, norm_biases], axis=1)
+    wa_local = jnp.concatenate([w_qkv, w_attn_out, jnp.pad(norm_cols, ((0, 0), (0, 124)))], axis=1)
+    wa = lax.all_gather(wa_local, both, axis=0, tiled=True)
+    norms = jnp.pad(wa[:, 4 * width : 4 * width + 4].astype(jnp.float32).T, ((0, 4), (0, 0)))
+    wa = wa[:, : 4 * width]
+    w1 = lax.all_to_all(w_in, "fsdp", split_axis=1, concat_axis=0, tiled=True)
+    w1 = lax.all_gather(w1, "dp", axis=0, tiled=True).reshape(EXPERTS, width, part)
+    w2 = lax.all_gather(w_out, "dp", axis=0, tiled=True).reshape(EXPERTS, part, width)
+
+    table = jnp.pad(hash_table, (0, (-hash_table.shape[0]) % 8192)).reshape(64, 128).T.astype(bf)
+    qkv, mixed, aug, hidden, xs, gs, pos, counts = front(
+        lengths, tokens, token_ids.reshape(1, slots), table, cotangent, wa, norms
+    )
+    expert_counts = lax.psum(counts[:EXPERTS, 0], both)
+    xs_all = lax.all_gather(xs, "fsdp", axis=0, tiled=True).reshape(plane, rp // GROUP + 1, GROUP, width)
+    gs_all = lax.all_gather(gs, "fsdp", axis=0, tiled=True).reshape(plane, rp // GROUP + 1, GROUP, width)
+    n16 = xs_all[:, rp // GROUP, :EXPERTS, 0].astype(jnp.int32).reshape(-1)
+    o_part, dx_part, gw1, gw2 = experts(n16, xs_all, gs_all, w1, w2)
+    os = lax.psum_scatter(o_part.reshape(plane * rp, width), "fsdp", scatter_dimension=0, tiled=True)
+    dxs = lax.psum_scatter(dx_part.reshape(plane * rp, width), "fsdp", scatter_dimension=0, tiled=True)
+    gw1 = lax.psum_scatter(gw1.reshape(EXPERTS * part, width), "dp", scatter_dimension=0, tiled=True)
+    gw2 = lax.psum_scatter(gw2.reshape(EXPERTS * part, width), "dp", scatter_dimension=0, tiled=True)
+    gw1 = lax.all_to_all(gw1, "fsdp", split_axis=1, concat_axis=0, tiled=True)
+    out, gx, gwa, gn = back(lengths, tokens, cotangent, hidden, qkv, mixed, aug, pos, dxs, os, wa, norms)
+    gwa = lax.psum_scatter(gwa, both, scatter_dimension=0, tiled=True).astype(jnp.float32)
+    gn = lax.psum_scatter(gn[:4].T, both, scatter_dimension=0, tiled=True)
+    return (
+        out, gx, gwa[:, : 3 * width], gwa[:, 3 * width :], gn[:, 0:2], gn[:, 2:4],
+        gw1.T.astype(jnp.float32), gw2.astype(jnp.float32), expert_counts,
+    )
+
+
 def solution(mesh):
     placed = (
         P(("dp", "fsdp"), None),
@@ -363,8 +938,9 @@
         P(("dp", "fsdp"), None),
         P(("dp", "fsdp"), None),
     )
+    by_plane = mesh.shape["dp"] == EXPERTS and mesh.shape["fsdp"] == 8
     return jax.shard_map(
-        body,
+        plane_body if by_plane else body,
         mesh=mesh,
         in_specs=placed,
         out_specs=(

time: 2100 us -> 856 us (0.41)
  matrix products: 548 us -> 0 us
  waiting for transfers between devices: 953 us -> 563 us
  blocking collectives: 257 us -> 103 us
  Pallas kernels: 0 us -> 147 us
  local copies, waits for them, and re-layouts: 160 us -> 14.6 us
  other arithmetic: 110 us -> 6.84 us
  loops' own time: 52.3 us -> 0 us
    dot_general x78 -> x0, matrix products: 548 us -> none  [the longest x9 86.5 us: compute(): jnp.einsum('tf,td->fd', activated.astype(jnp.bfloat16), grad_block, prefe...]
    reduce_scatter x4, waiting for transfers between devices: 797 us -> 257 us  [the longest x1 101 us: plane_body(): lax.psum_scatter(dx_part.reshape(plane * rp, width), 'fsdp', scatter_dime...]
    all_gather x4 -> x5, waiting for transfers between devices: 153 us -> 303 us  [the longest x1 76.9 us: plane_body(): lax.all_gather(gs, 'fsdp', axis=0, tiled=True)]
    pallas_call x0 -> x3, Pallas kernels: none -> 147 us  [the longest x1 56.5 us: back(): pl.pallas_call(back_kernel, out_shape=(jax.ShapeDtypeStruct((slots, width...]
    psum x1, blocking collectives: 135 us -> 45.7 us  [plane_body(): expert_counts = lax.psum(counts[:EXPERTS, 0], both)]
    all_gather x2 -> x0, blocking collectives: 79.5 us -> none  [the longest x1 43 us: body(): lax.all_gather(norm_gains, ('dp', 'fsdp'), axis=0, tiled=True)]
    dynamic_slice x96 -> x0, local copies, waits for them, and re-layouts: 57.9 us -> none  [expert_forward(): final_state, _ = lax.scan(visit, start_state, table)]
    another operation x26 -> x0, loops' own time: 52.3 us -> none  [the longest x24 35.8 us: visit(): return (lax.cond(live, compute, lambda same: same, state), None)]
  transfers between devices with their start and end apart: 8 -> 11, of which waited for: 5 -> 8; matrix products, arithmetic and copies ran while one was open for 9% -> 1% of each run, Pallas kernels for 0% -> 7%
where the time goes in v1:
time: 856 us; the launch traced here: 854 us
  waiting for transfers between devices  563 us (66%)
  Pallas kernels  147 us (17%)
  blocking collectives  103 us (12%)
  between operations  14.9 us (2%)
  local copies, waits for them, and re-layouts  14.6 us (2%)
    reduce_scatter x1, waiting for transfers between devices, plane_body(): lax.psum_scatter(dx_part.reshape(plane * rp, width), 'fsdp', scatter_dime...  101 us
    reduce_scatter x1, waiting for transfers between devices, plane_body(): lax.psum_scatter(o_part.reshape(plane * rp, width), 'fsdp', scatter_dimen...  95.7 us
    all_gather x1, waiting for transfers between devices, plane_body(): lax.all_gather(gs, 'fsdp', axis=0, tiled=True)  76.9 us
    all_gather x1, waiting for transfers between devices, plane_body(): wa = lax.all_gather(wa_local, both, axis=0, tiled=True)  66.8 us
    reduce_scatter x1, waiting for transfers between devices, plane_body(): lax.psum_scatter(gwa, both, scatter_dimension=0, tiled=True)  60.4 us
    all_gather x1, waiting for transfers between devices, plane_body(): lax.all_gather(xs, 'fsdp', axis=0, tiled=True)  57.9 us
    pallas_call x1, Pallas kernels, back(): pl.pallas_call(back_kernel, out_shape=(jax.ShapeDtypeStruct((slots, width...  56.5 us
    all_gather x1, waiting for transfers between devices, plane_body(): lax.all_gather(w1, 'dp', axis=0, tiled=True).reshape(EXPERTS, width, part)  50.8 us
  transfers between devices with their start and end apart: 11, of which 8 were waited for; matrix products, arithmetic and copies ran while one was open for 1% of the time, Pallas kernels for 7%

profile of v1, /device:TPU:0, one launch (start us, length us, event | category | flops | bytes accessed | tf_op | source)
XLA Modules:
  0.0 853.9 jit_solution(8946100865544827934)
XLA Ops:
  7.2 0.0 all-gather.6.cloned.1.call-start
  7.2 0.7 pad_maximum_fusion
  7.9 0.1 copy.65
  8.0 1.6 fusion.1
  9.6 0.0 all-gather.6.cloned.1.call-update
  9.6 0.0 all-gather.8.cloned.1.call-start
  10.3 0.8 convert.11
  11.1 0.7 copy.54
  11.8 66.8 %all-gather.6.cloned.1.call-done = bf16[768,3200]{1,0:T(8,128)(2,1)} async-done(((bf16[24,3200]{1,0:T(8,128)(2,1)}), bf16[768,3200]{1,0:T(8,128)(2,1)}) %all-gather.6.cloned.1.call-update) | async-done | bytes 4915216 | tf_op jit(solution)/shard_map/all_gather | solution.py:897
  78.6 0.9 slice.37
  79.6 0.1 copy.64
  79.7 0.6 pad_convert_fusion.norms_ref
  80.3 4.8 slice.36.wa_ref
  85.1 42.4 %front.1 = (bf16[1024,2304]{1,0:T(8,128)(2,1)}, bf16[1024,768]{1,0:T(8,128)(2,1)}, bf16[12,1024,128]{2,1,0:T(8,128)(2,1)}, f32[1024,768]{1,0:T(8,128)}, bf16[110...) custom-call(s32[1]{0:T(128)S(6)} %copy.70.len_ref, ...), custom_call_target="tpu_custom_call" | custom-call | tf_op jit(solution)/shard_map/front/pallas_call | solution.py:518
  127.5 0.0 all-gather.8.cloned.1.call-update
  127.5 0.0 all-gather.14.cloned.1.call-start
  127.6 0.7 all-gather.14.cloned.1.call-update
  128.3 0.0 all-gather.12.cloned.1.call-start
  128.3 0.3 copy-done
  128.6 0.1 copy.69
  128.6 17.3 %all_to_all.32 = bf16[96,8,384]{2,0,1:T(8,128)(2,1)} all-to-all(bf16[96,8,384]{2,0,1:T(8,128)(2,1)S(1)} %bitcast.42), channel_id=1, replica_groups=mesh['dp'=4,'fsdp'=8] {'fsdp'}, dimensions={1} | all-to-all | bytes 1179648 | tf_op jit(solution)/shard_map/all_to_all | solution.py:900
  145.9 0.0 all-gather.12.cloned.1.call-update
  146.0 0.0 all-gather.10.cloned.1.call-start
  146.0 0.5 all-gather.10.cloned.1.call-update
  146.6 0.0 reduce-scatter.11.cloned.1.call-start
  146.6 57.9 %all-gather.8.cloned.1.call-done = bf16[8832,768]{1,0:T(8,128)(2,1)} async-done(((bf16[1104,768]{1,0:T(8,128)(2,1)}), bf16[8832,768]{1,0:T(8,128)(2,1)}) %all-gather.8.cloned.1.call-update) | async-done | bytes 13565968 | tf_op jit(solution)/shard_map/all_gather | solution.py:909
  204.5 0.9 convert_reduce_fusion
  205.4 0.6 reshape.68.n_ref
  206.0 50.6 %all-gather.14.cloned.1.call-done = bf16[1536,768]{1,0:T(8,128)(2,1)} async-done(((bf16[384,768]{1,0:T(8,128)(2,1)}), bf16[1536,768]{1,0:T(8,128)(2,1)}) %all-gather.14.cloned.1.call-update) | async-done | bytes 2359312 | tf_op jit(solution)/shard_map/all_gather | solution.py:902
  256.6 50.8 %all-gather.12.cloned.1.call-done = bf16[3072,384]{1,0:T(8,128)(2,1)} async-done(((bf16[768,384]{1,0:T(8,128)(2,1)}), bf16[3072,384]{1,0:T(8,128)(2,1)}) %all-gather.12.cloned.1.call-update) | async-done | bytes 2359312 | tf_op jit(solution)/shard_map/all_gather | solution.py:901
  307.4 76.9 %all-gather.10.cloned.1.call-done = bf16[8832,768]{1,0:T(8,128)(2,1)} async-done(((bf16[1104,768]{1,0:T(8,128)(2,1)}), bf16[8832,768]{1,0:T(8,128)(2,1)}) %all-gather.10.cloned.1.call-update) | async-done | bytes 13565968 | tf_op jit(solution)/shard_map/all_gather | solution.py:910
  384.2 48.0 %experts.1 = (bf16[8,68,16,768]{3,2,1,0:T(8,128)(2,1)}, bf16[8,68,16,768]{3,2,1,0:T(8,128)(2,1)}, bf16[4,384,768]{2,1,0:T(8,128)(2,1)}, bf16[4,384,768]{2,1,0:T(8,128)(2,1)}) custom-call(s32[32]{0:T(128)} %reshape.68.n_ref, bf16[8,69,16,768]{3,2,1,0:T(8,128)(2,1)} %bitcast.33, bf16[8,69,16,768]{3,2,1,0:T(8,128)(2,1)} %bitcast.34, ...), custom_call_target="tpu_custom_call" | custom-call | tf_op jit(solution)/shard_map/experts/pallas_call | solution.py:719
  432.2 0.0 reduce-scatter.11.cloned.1.call-update
  432.2 0.0 reduce-scatter.9.cloned.1.call-start
  432.3 0.7 reduce-scatter.9.cloned.1.call-update
  433.0 0.0 reduce-scatter.17.cloned.1.call-start
  433.0 0.7 reduce-scatter.17.cloned.1.call-update
  433.7 0.0 reduce-scatter.15.cloned.1.call-start
  433.8 0.7 reduce-scatter.15.cloned.1.call-update
  434.4 0.2 reduce-scatter.13.cloned.1.call-start
  434.7 95.7 %reduce-scatter.11.cloned.1.call-done.os_ref = bf16[1088,768]{1,0:T(8,128)(2,1)} async-done(((bf16[8704,768]{1,0:T(8,128)(2,1)}), bf16[1088,768]{1,0:T(8,128)(2,1)}) %reduce-scatter.11.cloned.1.call-update) | async-done | bytes 1671184 | tf_op jit(solution)/shard_map/reduce_scatter | solution.py:913
  530.4 100.6 %reduce-scatter.9.cloned.1.call-done.dxs_ref = bf16[1088,768]{1,0:T(8,128)(2,1)} async-done(((bf16[8704,768]{1,0:T(8,128)(2,1)}), bf16[1088,768]{1,0:T(8,128)(2,1)}) %reduce-scatter.9.cloned.1.call-update) | async-done | bytes 1671184 | tf_op jit(solution)/shard_map/reduce_scatter | solution.py:914
  631.1 56.5 %back.1 = (bf16[1024,768]{1,0:T(8,128)(2,1)}, f32[1024,768]{1,0:T(8,128)}, bf16[768,3072]{1,0:T(8,128)(2,1)}, f32[8,768]{1,0:T(8,128)}) custom-call(s32[1]{0:T(128)S(6)} %copy.70.len_ref, bf16[1024,768]{1,0:T(8,128)(2,1)} %x_ref.3, bf16[1024,768]{1,0:T(8,128)(2,1)} %g_ref.3, f32[1024,768]{1,0:T(8,128)} %get-tuple-element.25.hidden_ref, ...), custom_call_target="tpu_custom_call" | custom-call | tf_op jit(solution)/shard_map/back/pallas_call | solution.py:857
  687.6 0.0 reduce-scatter.13.cloned.1.call-update
  687.6 0.0 copy-start.2
  687.6 0.0 reduce-scatter.17.cloned.1.call-done
  687.7 2.1 copy.63
  689.8 3.5 all-to-all-start.1
  693.3 0.0 copy-done.2
  693.3 0.1 slice_reduce_fusion
  693.5 45.7 %psum.7 = s32[4]{0:T(128)} all-reduce(s32[4]{0:T(128)S(1)} %slice_reduce_fusion), channel_id=1, replica_groups=mesh['dp'=4,'fsdp'=8] {'dp','fsdp'}, use_global_device_ids=true, to_apply=%region_6.7 | all-reduce | flops 4 | bytes 32 | tf_op jit(solution)/shard_map/psum | solution.py:908
  739.2 0.0 reduce-scatter.15.cloned.1.call-done
  739.2 2.2 convert_element_type.44
  741.3 0.0 copy-start.1
  741.4 0.0 all-to-all-done.1
  741.4 0.1 convert_bitcast_fusion
  741.4 1.1 copy.67
  742.6 0.0 copy-done.1
  742.6 40.4 %all-reduce.3 = f32[768,4]{0,1:T(4,128)S(1)} all-reduce(f32[768,4]{0,1:T(4,128)S(1)} %slice_bitcast_fusion), channel_id=5, replica_groups=mesh['dp'=4,'fsdp'=8] {'dp','fsdp'}, use_global_device_ids=true, to_apply=%region_3.4.clone | all-reduce | flops 3072 | bytes 24576
  783.0 0.1 constant_dynamic-slice_fusion
  783.1 0.6 fusion.2
  783.6 60.4 %reduce-scatter.13.cloned.1.call-done = bf16[24,3072]{1,0:T(8,128)(2,1)} async-done(((bf16[768,3072]{1,0:T(8,128)(2,1)}), bf16[24,3072]{1,0:T(8,128)(2,1)}) %reduce-scatter.13.cloned.1.call-update) | async-done | bytes 147472 | tf_op jit(solution)/shard_map/reduce_scatter | solution.py:919
  844.1 1.4 slice.40
  845.5 1.6 slice.39
  (3 shorter events, 0.0 us)
Async XLA Ops:
  7.2 71.4 %all-gather.6.cloned.1.call-start = ((), (), s32[]{:S(2)}) async-start(), calls=%async_computation.7 | async-start | bytes 5068800 | tf_op jit(solution)/shard_map/all_gather | solution.py:897
  9.6 194.9 %all-gather.8.cloned.1.call-start = ((), (), s32[]{:S(2)}) async-start(), calls=%async_computation.8 | async-start | bytes 15261696 | tf_op jit(solution)/shard_map/all_gather | solution.py:909
  127.5 1.1 copy-start
  127.5 129.1 %all-gather.14.cloned.1.call-start = ((), (), s32[]{:S(2)}) async-start(), calls=%async_computation.11 | async-start | bytes 2949120 | tf_op jit(solution)/shard_map/all_gather | solution.py:902
  128.3 179.1 %all-gather.12.cloned.1.call-start = ((), (), s32[]{:S(2)}) async-start(), calls=%async_computation.10 | async-start | bytes 2949120 | tf_op jit(solution)/shard_map/all_gather | solution.py:901
  146.0 238.3 %all-gather.10.cloned.1.call-start = ((), (), s32[]{:S(2)}) async-start(), calls=%async_computation.9 | async-start | bytes 15261696 | tf_op jit(solution)/shard_map/all_gather | solution.py:910
  146.6 383.9 %reduce-scatter.11.cloned.1.call-start = ((), (), s32[]{:S(2)}) async-start(), calls=%async_computation.13 | async-start | bytes 15040512 | tf_op jit(solution)/shard_map/reduce_scatter | solution.py:913
  432.2 198.9 %reduce-scatter.9.cloned.1.call-start = ((), (), s32[]{:S(2)}) async-start(), calls=%async_computation.12 | async-start | bytes 15040512 | tf_op jit(solution)/shard_map/reduce_scatter | solution.py:914
  433.0 254.7 %reduce-scatter.17.cloned.1.call-start = ((), (), s32[]{:S(2)}) async-start(), calls=%async_computation.16 | async-start | bytes 2949120
  433.7 305.5 %reduce-scatter.15.cloned.1.call-start = ((), (), s32[]{:S(2)}) async-start(), calls=%async_computation.15 | async-start | bytes 2949120 | tf_op jit(solution)/shard_map/reduce_scatter | solution.py:916
  434.4 409.6 %reduce-scatter.13.cloned.1.call-start = ((), (), s32[]{:S(2)}) async-start(), calls=%async_computation.14 | async-start | bytes 4866048 | tf_op jit(solution)/shard_map/reduce_scatter | solution.py:919
  687.6 5.7 copy-start.2
  689.8 51.6 %all-to-all-start.1 = ((bf16[384,8,96]{0,2,1:T(8,128)(2,1)}), bf16[384,8,96]{0,2,1:T(8,128)(2,1)S(1)}, u32[]{:S(2)}, u32[]{:S(2)}) async-start(bf16[384,8,96]{0,2,1:T(8,128)(2,1)} %bitcast.17), calls=%async_computation.4 | async-start | bytes 1179648 | tf_op jit(solution)/shard_map/all_to_all | solution.py:917
  741.3 1.2 copy-start.1
Sparse Core Ops, SparseCore 0:
  11.5 67.0 all-gather.5
  127.6 76.8 all-gather.7
  206.1 50.4 all-gather.13
  258.0 49.2 all-gather.11
  309.1 75.0 all-gather.9
  432.3 98.0 reduce-scatter.10
  534.5 96.5 reduce-scatter.8
  633.4 47.9 reduce-scatter.16
  683.7 48.3 reduce-scatter.14
  737.5 106.5 reduce-scatter.12

commit v2 on v1

--- a/solution.py
+++ b/solution.py
@@ -1,3 +1,5 @@
+import functools
+
 import jax
 import jax.numpy as jnp
 from jax import lax
@@ -412,20 +414,223 @@
     return place, counts, groups
 
 
+MESH = pl.DeviceIdType.MESH
+HALF = 1664
+WIDE = 2 * HALF
+
+
+class Place:
+    def __init__(self):
+        self.z = lax.axis_index("dp")
+        f = lax.axis_index("fsdp")
+        self.y = f // 4
+        self.x = (f // 2) % 2
+        self.c = f % 2
+
+    def at(self, z=None, y=None, x=None, c=None):
+        z = self.z if z is None else z
+        y = self.y if y is None else y
+        x = self.x if x is None else x
+        c = self.c if c is None else c
+        return (z, 4 * y + 2 * x + c)
+
+    def greet(self, peers):
+        barrier = pltpu.get_barrier_semaphore()
+        for peer in peers:
+            pl.semaphore_signal(barrier, inc=1, device_id=peer, device_id_type=MESH)
+        pl.semaphore_wait(barrier, len(peers))
+
+
+def push(src, dst, send, recv, peer):
+    return pltpu.make_async_remote_copy(
+        src_ref=src, dst_ref=dst, send_sem=send, recv_sem=recv, device_id=peer, device_id_type=MESH
+    )
+
+
 def front_kernel(
-    len_ref, x_ref, ids_ref, table_ref, g_ref, wa_ref, norms_ref,
-    qkv_ref, mixed_ref, aug_ref, hidden_ref, xs_ref, gs_ref, pos_ref, counts_ref,
-    perm_ref, normed_ref, qa_ref, ka_ref, va_ref,
+    len_ref, x_ref, ids_ref, table_ref, g_ref, local_ref, win_ref, wout_ref,
+    qkv_ref, mixed_ref, aug_ref, hidden_ref, xs_ref, gs_ref, w_ref, wa_ref, norms_ref, pos_ref, counts_ref,
+    perm_ref, normed_ref, qa_ref, ka_ref, va_ref, tokx_ref, tokg_ref, sib_ref,
+    sem0, sz, rz, sy, ry, sx, rx, sd, rd, ss, rs,
+    tok_local, tok_send, tok_recv,
+    lane_local, lane_send, lane_recv, up_send, down_send, line_recv, y_send, y_recv,
 ):
     slots, width = x_ref.shape
     heads = width // HEAD_DIM
     rp = padded_rows(slots)
     length = len_ref[0]
+    me = Place()
+    z, y, x, c = me.z, me.y, me.x, me.c
+    depth = 4
+    sibling, beside, across = me.at(c=1 - c), me.at(x=1 - x), me.at(y=1 - y)
+    me.greet([sibling, beside, across, me.at(x=1 - x, c=1 - c)] + [me.at(z=z ^ k) for k in range(1, depth)])
+
+    first = push(local_ref, sib_ref, sem0.at[0], sem0.at[1], sibling)
+    first.start()
+
+    def block(zz, yy, xx):
+        rows = pl.ds(pl.multiple_of(48 * (4 * zz + 2 * yy + xx), 48), 48)
+        return wa_ref.at[rows, pl.ds(pl.multiple_of(c * HALF, 128), HALF)]
+
+    def share(zz, yy, xx, send, recv, peer):
+        ref = block(zz, yy, xx)
+        return push(ref, ref, send, recv, peer)
+
+    def z_copy(k, source):
+        return share(source, y, x, sz.at[k - 1], rz.at[source], me.at(z=z ^ k))
+
+    def y_copy(zz, source_y):
+        return share(zz, source_y, x, sy.at[zz], ry.at[zz], across)
+
+    def x_copy(zz, source_x):
+        return share(zz, y, source_x, sx.at[zz], rx.at[zz], beside)
+
+    def d_copy_x(zz, yy, xx):
+        return share(zz, yy, xx, sd.at[zz], rd.at[zz], beside)
+
+    def d_copy_y(zz, yy, xx):
+        return share(zz, yy, xx, sd.at[zz], rd.at[zz], across)
+
+    def s_copy(zz, side):
+        ref = wa_ref.at[pl.ds(pl.multiple_of(192 * zz, 192), 192), pl.ds(pl.multiple_of(side * HALF, 128), HALF)]
+        return push(ref, ref, ss.at[zz], rs.at[zz], sibling)
+
+    part = wout_ref.shape[0]
+    rows_in = win_ref.shape[0]
+    lanes = [(1 - x, c), (x, 1 - c), (1 - x, 1 - c)]
+
+    def lane_cols(b, xx, cc):
+        return win_ref.at[:, pl.ds(pl.multiple_of(part * (4 * b + 2 * xx + cc), 128), part)]
+
+    def lane_home(b, xx, cc):
+        return w_ref.at[0, z, y, pl.ds(pl.multiple_of(rows_in * (2 * xx + cc), rows_in), rows_in), pl.ds(b * part, part)]
+
+    def lane_copy(i, b, arrive):
+        xx, cc = lanes[i]
+        home = lane_home(b, xx, cc) if arrive else lane_home(b, x, c)
+        return push(lane_cols(b, xx, cc), home, lane_send.at[i, b], lane_recv.at[i, b], me.at(x=xx, c=cc))
+
+    def lane_own(b):
+        return pltpu.make_async_copy(lane_cols(b, x, c), lane_home(b, x, c), lane_local.at[b])
+
+    own_out = pltpu.make_async_copy(wout_ref, w_ref.at[1, z, y], lane_local.at[2])
+
+    def shard(k, zz, yy):
+        return w_ref.at[k, zz, yy]
+
+    def up_copy(k, zz):
+        return push(shard(k, zz, y), shard(k, zz, y), up_send.at[k, zz], line_recv.at[k, zz], me.at(z=jnp.minimum(z + 1, depth - 1)))
+
+    def down_copy(k, zz):
+        return push(shard(k, zz, y), shard(k, zz, y), down_send.at[k, zz], line_recv.at[k, zz], me.at(z=jnp.maximum(z - 1, 0)))
+
+    def over_copy(k, zz, yy):
+        return push(shard(k, zz, yy), shard(k, zz, yy), y_send.at[k, zz], y_recv.at[k, zz], across)
+
+    def spread(k):
+        @pl.when(z < depth - 1)
+        def _():
+            up_copy(k, z).start()
+
+        @pl.when(z > 0)
+        def _():
+            down_copy(k, z).start()
+
+        over_copy(k, z, y).start()
+
+    def relay(k, s):
+        @pl.when(z >= s)
+        def _():
+            up_copy(k, z - s).wait_recv()
+
+            @pl.when(z < depth - 1)
+            def _():
+                up_copy(k, z - s).start()
+
+            over_copy(k, z - s, y).start()
+
+        @pl.when(z + s < depth)
+        def _():
+            down_copy(k, z + s).wait_recv()
+
+            @pl.when(z > 0)
+            def _():
+                down_copy(k, z + s).start()
+
+            over_copy(k, z + s, y).start()
+
+    def weights_start():
+        for i in range(3):
+            for b in range(2):
+                lane_copy(i, b, False).start()
+        spread(1)
+
+    def weights_lane():
+        for i in range(3):
+            for b in range(2):
+                lane_copy(i, b, True).wait_recv()
+        for b in range(2):
+            lane_own(b).wait()
+        spread(0)
+
+    ticks = [weights_lane] + [functools.partial(relay, k, s) for s in range(1, depth) for k in (1, 0)]
+
+    def weights_end():
+        for k in (1, 0):
+            for zz in range(depth):
+                over_copy(k, zz, 1 - y).wait()
+                for copy, stop in ((up_copy, depth - 1), (down_copy, 0)):
+                    inside = (zz <= z) if stop else (zz >= z)
+
+                    @pl.when(inside & (z != stop))
+                    def _():
+                        copy(k, zz).wait_send()
+
+        for i in range(3):
+            for b in range(2):
+                lane_copy(i, b, False).wait_send()
+
+    mine = 2 * x + c
+
+    def tok_copies(k, scratch, far_ref):
+        own = pltpu.make_async_copy(scratch, far_ref.at[mine], tok_local.at[k])
+        near = push(scratch, far_ref.at[mine], tok_send.at[k, 0], tok_recv.at[k, 0], sibling)
+        far = push(scratch, far_ref.at[mine], tok_send.at[k, 1], tok_recv.at[k, 1], beside)
+        slot = far_ref.at[2 * (1 - x) + c]
+        onward = push(slot, slot, tok_send.at[k, 2], tok_recv.at[k, 2], sibling)
+        return own, near, far, onward
+
+    x_copies = tok_copies(0, tokx_ref, xs_ref)
+    g_copies = tok_copies(1, tokg_ref, gs_ref)
+
+    first.wait_recv()
+    zero_core = c == 0
+    own_cols = pl.ds(pl.multiple_of(c * HALF, 128), HALF)
+    local = local_ref[0:24, own_cols]
+    other = sib_ref[0:24, own_cols]
+    own_rows = pl.ds(pl.multiple_of(48 * (4 * z + 2 * y + x), 48), 48)
+    wa_ref[own_rows, own_cols] = jnp.concatenate(
+        [jnp.where(zero_core, local, other), jnp.where(zero_core, other, local)], axis=0
+    )
+    for k in range(1, depth):
+        z_copy(k, z).start()
+    y_copy(z, y).start()
+    x_copy(z, x).start()
+    for b in range(2):
+        lane_own(b).start()
+    own_out.start()
 
     place, counts, groups = routing(ids_ref[...], table_ref[...], length, perm_ref)
+    place_i = place.astype(jnp.int32)
     pos_ref[...] = jnp.broadcast_to(place, (128, slots)).T
     counts_ref[...] = jnp.broadcast_to(counts, (8, 128)).astype(jnp.int32)
-    place_i = place.astype(jnp.int32)
+
+    for k in range(1, depth):
+        zz = z ^ k
+        z_copy(k, zz).wait_recv()
+        y_copy(zz, y).start()
+        x_copy(zz, x).start()
+
     step = rp // 4
 
     @pl.loop(0, 4)
@@ -434,27 +639,63 @@
         perm_ref[pl.ds(base, step), :] = (
             iota((step, slots), 0) + base == place_i
         ).astype(jnp.bfloat16)
-        gs_ref[pl.ds(base, step), :] = mul(perm_ref[pl.ds(base, step), :], g_ref[...]).astype(jnp.bfloat16)
+
+    for k in range(depth):
+        zz = z ^ k
+        y_copy(zz, 1 - y).wait_recv()
+        x_copy(zz, 1 - x).wait_recv()
+
+        @pl.when(zz % 2 == 0)
+        def _():
+            d_copy_x(zz, 1 - y, x).start()
+
+        @pl.when(zz % 2 == 1)
+        def _():
+            d_copy_y(zz, y, 1 - x).start()
+
+    own_out.wait()
+    weights_start()
+
+    @pl.loop(0, 4)
+    def _(i):
+        rows = pl.ds(i * step, step)
+        tokg_ref[rows, :] = mul(perm_ref[rows, :], g_ref[...]).astype(jnp.bfloat16)
 
     tail = jnp.broadcast_to(jnp.concatenate([groups, groups], axis=0), (GROUP, width)).astype(jnp.bfloat16)
-    xs_ref[rp : rp + GROUP, :] = tail
-    gs_ref[rp : rp + GROUP, :] = tail
+    tokx_ref[rp : rp + GROUP, :] = tail
+    tokg_ref[rp : rp + GROUP, :] = tail
+
+    for k in range(depth):
+        zz = z ^ k
+        d_copy_x(zz, 1 - y, 1 - x).wait_recv()
+        s_copy(zz, c).start()
+    for k in range(depth):
+        s_copy(z ^ k, 1 - c).wait_recv()
+    for copy in g_copies[:3]:
+        copy.start()
+
+    cols_t = wa_ref[:, 2 * width : 2 * width + 128].astype(jnp.float32).T
+    norms_ref[...] = cols_t[0:8, :]
 
     @pl.loop(0, slots // ROWS)
     def _(i):
         rows = pl.ds(i * ROWS, ROWS)
         normal, _ = layer_stats(x_ref[rows, :].astype(jnp.float32))
         normed = (normal * norms_ref[0:1, :] + norms_ref[2:3, :]).astype(jnp.bfloat16)
-        for c in range(3):
-            cols = slice(c * width, (c + 1) * width)
-            qkv_ref[rows, cols] = mul(normed, wa_ref[:, cols]).astype(jnp.bfloat16)
+        for part_i, start in enumerate((0, width, HALF)):
+            cols = slice(part_i * width, (part_i + 1) * width)
+            qkv_ref[rows, cols] = mul(normed, wa_ref[:, start : start + width]).astype(jnp.bfloat16)
 
     lane = iota((slots, 128), 1)
     key_bias = jnp.where(iota((slots, 128), 0) < length, 0.0, NEGATIVE).astype(jnp.bfloat16)
     causal = iota((ROWS, ROWS), 1) <= iota((ROWS, ROWS), 0)
     lane_b = iota((ROWS, 128), 1)
-
-    @pl.loop(0, heads // 2)
+    pairs = heads // 2
+    slots_for = [[] for _ in range(pairs)]
+    for i, tick in enumerate(ticks[:pairs]):
+        slots_for[i].append(tick)
+
+    @pl.loop(0, pairs)
     def _(p):
         cols = pl.ds(p * 128, 128)
         q = qkv_ref[:, cols].astype(jnp.float32) * (HEAD_DIM ** -0.5 * LOG2E)
@@ -464,7 +705,6 @@
         v = qkv_ref[:, pl.ds(2 * width + p * 128, 128)]
         zero = jnp.zeros_like(q_hi)
         one = jnp.ones_like(q_hi)
-        sides = []
         for half in range(2):
             own = own_lanes(lane, half)
             extra = extra_lane(half)
@@ -487,19 +727,24 @@
                 total = pltpu.roll(out, HEAD_DIM, 1)
                 outs.append(out / total)
                 minus = -(top + jnp.log2(out))
-                a, b, c = three_parts(minus)
+                a, b, d = three_parts(minus)
                 extra = extra_lane(half)
                 seen = qa_ref[half, rows, 128:256]
                 seen = jnp.where(lane_b == extra + 1, a, seen)
                 seen = jnp.where(lane_b == extra + 2, b, seen)
-                seen = jnp.where(lane_b == extra + 3, c, seen)
+                seen = jnp.where(lane_b == extra + 3, d, seen)
                 aug_ref[2 * p + half, rows, :] = seen
             mixed_ref[rows, cols] = jnp.where(lane_b < HEAD_DIM, outs[0], outs[1]).astype(jnp.bfloat16)
+        for i in range(pairs):
+            @pl.when(p == i)
+            def _():
+                for tick in slots_for[i]:
+                    tick()
 
     @pl.loop(0, slots // ROWS)
     def _(i):
         rows = pl.ds(i * ROWS, ROWS)
-        hidden = x_ref[rows, :].astype(jnp.float32) + mul(mixed_ref[rows, :], wa_ref[:, 3 * width :])
+        hidden = x_ref[rows, :].astype(jnp.float32) + mul(mixed_ref[rows, :], wa_ref[:, HALF + width : HALF + 2 * width])
         hidden_ref[rows, :] = hidden
         normal, _ = layer_stats(hidden)
         normed_ref[rows, :] = (normal * norms_ref[1:2, :] + norms_ref[3:4, :]).astype(jnp.bfloat16)
@@ -507,38 +752,75 @@
     @pl.loop(0, 4)
     def _(i):
         rows = pl.ds(i * step, step)
-        xs_ref[rows, :] = mul(perm_ref[rows, :], normed_ref[...]).astype(jnp.bfloat16)
-
-
-def front(length, x, ids, table, g, wa, norms):
+        tokx_ref[rows, :] = mul(perm_ref[rows, :], normed_ref[...]).astype(jnp.bfloat16)
+
+    for copy in x_copies[:3]:
+        copy.start()
+    g_copies[2].wait_recv()
+    g_copies[3].start()
+    for tick in ticks[pairs:]:
+        tick()
+    x_copies[2].wait_recv()
+    x_copies[3].start()
+    weights_end()
+    for own, near, far, onward in (x_copies, g_copies):
+        own.wait()
+        near.wait()
+        far.wait_send()
+        onward.wait()
+    first.wait_send()
+    for k in range(1, depth):
+        z_copy(k, z).wait_send()
+    for zz in range(depth):
+        y_copy(zz, y).wait_send()
+        x_copy(zz, x).wait_send()
+        d_copy_x(zz, y, x).wait_send()
+        s_copy(zz, c).wait_send()
+
+
+def front(length, x, ids, table, g, local, w_in, w_out):
     slots, width = x.shape
     rp = padded_rows(slots)
+    part = w_out.shape[0]
     bf = jnp.bfloat16
+    f32 = jnp.float32
     whole = pl.BlockSpec(memory_space=pltpu.VMEM)
+    far = pl.BlockSpec(memory_space=pl.ANY)
+    dma = pltpu.SemaphoreType.DMA
     return pl.pallas_call(
         front_kernel,
         out_shape=(
             jax.ShapeDtypeStruct((slots, 3 * width), bf),
             jax.ShapeDtypeStruct((slots, width), bf),
             jax.ShapeDtypeStruct((HEADS, slots, 128), bf),
-            jax.ShapeDtypeStruct((slots, width), jnp.float32),
-            jax.ShapeDtypeStruct((rp + GROUP, width), bf),
-            jax.ShapeDtypeStruct((rp + GROUP, width), bf),
-            jax.ShapeDtypeStruct((slots, 128), jnp.float32),
+            jax.ShapeDtypeStruct((slots, width), f32),
+            jax.ShapeDtypeStruct((4, rp + GROUP, width), bf),
+            jax.ShapeDtypeStruct((4, rp + GROUP, width), bf),
+            jax.ShapeDtypeStruct((2, EXPERTS, 2, part, width), bf),
+            jax.ShapeDtypeStruct((width, WIDE), bf),
+            jax.ShapeDtypeStruct((8, width), f32),
+            jax.ShapeDtypeStruct((slots, 128), f32),
             jax.ShapeDtypeStruct((8, 128), jnp.int32),
         ),
-        in_specs=[pl.BlockSpec(memory_space=pltpu.SMEM)] + [whole] * 6,
-        out_specs=tuple([whole] * 8),
+        in_specs=[pl.BlockSpec(memory_space=pltpu.SMEM)] + [whole] * 5 + [far] * 2,
+        out_specs=(whole, whole, whole, whole, far, far, far, whole, whole, whole, whole),
         scratch_shapes=[
             pltpu.VMEM((rp, slots), bf),
             pltpu.VMEM((slots, width), bf),
             pltpu.VMEM((2, slots, 256), bf),
             pltpu.VMEM((2, slots, 256), bf),
             pltpu.VMEM((2, slots, 128), bf),
+            pltpu.VMEM((rp + GROUP, width), bf),
+            pltpu.VMEM((rp + GROUP, width), bf),
+            pltpu.VMEM((32, WIDE), bf),
+            dma((2,)), dma((3,)), dma((4,)), dma((4,)), dma((4,)), dma((4,)), dma((4,)), dma((4,)), dma((4,)),
+            dma((4,)), dma((4,)),
+            dma((2,)), dma((2, 3)), dma((2, 3)),
+            dma((3,)), dma((3, 2)), dma((3, 2)), dma((2, 4)), dma((2, 4)), dma((2, 4)), dma((2, 4)), dma((2, 4)),
         ],
-        compiler_params=pltpu.CompilerParams(vmem_limit_bytes=56 * MIB),
+        compiler_params=pltpu.CompilerParams(vmem_limit_bytes=56 * MIB, collective_id=0, has_side_effects=True),
         name="front",
-    )(length, x, ids, table, g, wa, norms)
+    )(length, x, ids, table, g, local, w_in, w_out)
 
 
 CHUNK = 32
@@ -678,7 +960,7 @@
         ob[slot] = mul(act, w2).astype(jnp.bfloat16).reshape(CHUNK, GROUP, width)
         db[slot] = mul(grad_pre, w1, NT).astype(jnp.bfloat16).reshape(CHUNK, GROUP, width)
         store(c, slot)
-        add1 = mul(grad_pre.T, x)
+        add1 = mul(x.T, grad_pre)
         add2 = mul(act.T, g)
 
         @pl.when(begin == 0)
@@ -720,13 +1002,13 @@
         experts_kernel,
         out_shape=(
             out_rows, out_rows,
-            jax.ShapeDtypeStruct((EXPERTS, hidden, width), bf),
+            jax.ShapeDtypeStruct((EXPERTS, width, hidden), bf),
             jax.ShapeDtypeStruct((EXPERTS, hidden, width), bf),
         ),
         in_specs=[pl.BlockSpec(memory_space=pltpu.SMEM), far, far, whole, whole],
         out_specs=(far, far, whole, whole),
         scratch_shapes=[pltpu.VMEM((2, CHUNK, GROUP, width), bf)] * 4
-        + [pltpu.VMEM((hidden, width), jnp.float32)] * 2
+        + [pltpu.VMEM((width, hidden), jnp.float32), pltpu.VMEM((hidden, width), jnp.float32)]
         + [pltpu.VMEM((groups - 1, GROUP, width), bf)]
         + [pltpu.SemaphoreType.DMA((2, 2)), pltpu.SemaphoreType.DMA((2, 2)), pltpu.SemaphoreType.DMA((2, sources))],
         compiler_params=pltpu.CompilerParams(vmem_limit_bytes=56 * MIB),
@@ -761,7 +1043,7 @@
         gx_ref[rows, :] = grad_hidden
         branch = grad_hidden.astype(jnp.bfloat16)
         branch_ref[rows, :] = branch
-        gmix_ref[rows, :] = mul(branch, wa_ref[:, 3 * width :], NT).astype(jnp.bfloat16)
+        gmix_ref[rows, :] = mul(branch, wa_ref[:, HALF + width : HALF + 2 * width], NT).astype(jnp.bfloat16)
 
     tr_ref[...] = mixed_ref[...].T
     tile = width // 3
@@ -834,7 +1116,9 @@
         rows = pl.ds(i * ROWS, ROWS)
         normal, scaled = layer_stats(x_ref[rows, :].astype(jnp.float32))
         branch_ref[rows, :] = (normal * norms_ref[0:1, :] + norms_ref[2:3, :]).astype(jnp.bfloat16)
-        grad = mul(gqkv_ref[rows, :], wa_ref[:, : 3 * width], NT)
+        grad = mul(gqkv_ref[rows, : 2 * width], wa_ref[:, : 2 * width], NT) + mul(
+            gqkv_ref[rows, 2 * width :], wa_ref[:, HALF : HALF + width], NT
+        )
         gn_ref[0:1, :] += jnp.sum(grad * normal, axis=0, keepdims=True)
         gn_ref[2:3, :] += jnp.sum(grad, axis=0, keepdims=True)
         gx_ref[rows, :] += norm_backward(grad, normal, scaled, norms_ref[0:1, :])
@@ -888,39 +1172,47 @@
     slots, width = tokens.shape
     bf = jnp.bfloat16
     both = ("dp", "fsdp")
-    plane = lax.axis_size("fsdp")
-    part = w_in.shape[1] // plane
     rp = padded_rows(slots)
+    part = w_out.shape[0]
 
     norm_cols = jnp.concatenate([norm_gains, norm_biases], axis=1)
-    wa_local = jnp.concatenate([w_qkv, w_attn_out, jnp.pad(norm_cols, ((0, 0), (0, 124)))], axis=1)
-    wa = lax.all_gather(wa_local, both, axis=0, tiled=True)
-    norms = jnp.pad(wa[:, 4 * width : 4 * width + 4].astype(jnp.float32).T, ((0, 4), (0, 0)))
-    wa = wa[:, : 4 * width]
-    w1 = lax.all_to_all(w_in, "fsdp", split_axis=1, concat_axis=0, tiled=True)
-    w1 = lax.all_gather(w1, "dp", axis=0, tiled=True).reshape(EXPERTS, width, part)
-    w2 = lax.all_gather(w_out, "dp", axis=0, tiled=True).reshape(EXPERTS, part, width)
-
+    local = jnp.concatenate(
+        [w_qkv[:, : 2 * width], jnp.pad(norm_cols, ((0, 0), (0, 124))), w_qkv[:, 2 * width :], w_attn_out], axis=1
+    )
+    local = jnp.pad(local, ((0, 32 - local.shape[0]), (0, WIDE - local.shape[1])))
     table = jnp.pad(hash_table, (0, (-hash_table.shape[0]) % 8192)).reshape(64, 128).T.astype(bf)
-    qkv, mixed, aug, hidden, xs, gs, pos, counts = front(
-        lengths, tokens, token_ids.reshape(1, slots), table, cotangent, wa, norms
+    qkv, mixed, aug, hidden, xs, gs, w, wa, norms, pos, counts = front(
+        lengths, tokens, token_ids.reshape(1, slots), table, cotangent, local, w_in, w_out
     )
     expert_counts = lax.psum(counts[:EXPERTS, 0], both)
-    xs_all = lax.all_gather(xs, "fsdp", axis=0, tiled=True).reshape(plane, rp // GROUP + 1, GROUP, width)
-    gs_all = lax.all_gather(gs, "fsdp", axis=0, tiled=True).reshape(plane, rp // GROUP + 1, GROUP, width)
-    n16 = xs_all[:, rp // GROUP, :EXPERTS, 0].astype(jnp.int32).reshape(-1)
-    o_part, dx_part, gw1, gw2 = experts(n16, xs_all, gs_all, w1, w2)
-    os = lax.psum_scatter(o_part.reshape(plane * rp, width), "fsdp", scatter_dimension=0, tiled=True)
-    dxs = lax.psum_scatter(dx_part.reshape(plane * rp, width), "fsdp", scatter_dimension=0, tiled=True)
-    gw1 = lax.psum_scatter(gw1.reshape(EXPERTS * part, width), "dp", scatter_dimension=0, tiled=True)
-    gw2 = lax.psum_scatter(gw2.reshape(EXPERTS * part, width), "dp", scatter_dimension=0, tiled=True)
-    gw1 = lax.all_to_all(gw1, "fsdp", split_axis=1, concat_axis=0, tiled=True)
+    xs = xs.reshape(4, rp // GROUP + 1, GROUP, width)
+    gs = gs.reshape(4, rp // GROUP + 1, GROUP, width)
+    n16 = xs[:, rp // GROUP, :EXPERTS, 0].astype(jnp.int32).reshape(-1)
+    w1 = w[0].reshape(EXPERTS, width, 2 * part)
+    w2 = w[1].reshape(EXPERTS, 2 * part, width)
+    o_part, dx_part, gw1, gw2 = experts(n16, xs, gs, w1, w2)
+    near = [[0, 1, 2, 3], [4, 5, 6, 7]]
+    over = [[0, 4], [1, 5], [2, 6], [3, 7]]
+    sum_near = lambda v: lax.psum_scatter(v, "fsdp", scatter_dimension=0, tiled=True, axis_index_groups=near)
+    os = sum_near(o_part.reshape(4 * rp, width))
+    dxs = sum_near(dx_part.reshape(4 * rp, width))
+
+    def sum_owners(v):
+        v = lax.psum_scatter(v.reshape(EXPERTS * 2 * part, width), "dp", scatter_dimension=0, tiled=True)
+        return lax.psum_scatter(v, "fsdp", scatter_dimension=0, tiled=True, axis_index_groups=over)
+
+    gw1 = sum_owners(gw1)
+    gw2 = sum_owners(gw2)
+    gw1 = lax.all_to_all(
+        gw1.reshape(4, part // 4, 2 * part), "fsdp", split_axis=0, concat_axis=0, tiled=True, axis_index_groups=near
+    )
+    gw1 = gw1.reshape(4, part // 4, 2, part).transpose(1, 2, 0, 3).reshape(part // 4, 8 * part)
     out, gx, gwa, gn = back(lengths, tokens, cotangent, hidden, qkv, mixed, aug, pos, dxs, os, wa, norms)
     gwa = lax.psum_scatter(gwa, both, scatter_dimension=0, tiled=True).astype(jnp.float32)
     gn = lax.psum_scatter(gn[:4].T, both, scatter_dimension=0, tiled=True)
     return (
         out, gx, gwa[:, : 3 * width], gwa[:, 3 * width :], gn[:, 0:2], gn[:, 2:4],
-        gw1.T.astype(jnp.float32), gw2.astype(jnp.float32), expert_counts,
+        gw1.astype(jnp.float32), gw2.astype(jnp.float32), expert_counts,
     )
 
 

time: 856 us -> 707 us (0.83)
  waiting for transfers between devices: 563 us -> 322 us
  Pallas kernels: 147 us -> 257 us
  blocking collectives: 103 us -> 83.2 us
    all_gather x5 -> x0, waiting for transfers between devices: 303 us -> none  [the longest x1 76.9 us: plane_body(): lax.all_gather(gs, 'fsdp', axis=0, tiled=True)]
    pallas_call x1, Pallas kernels: 42.4 us -> 155 us  [front(): pl.pallas_call(front_kernel, out_shape=(jax.ShapeDtypeStruct((slots, 3 *...]
    reduce_scatter x3 -> x6, waiting for transfers between devices: 196 us -> 305 us  [the longest x2 177 us: sum_owners(): lax.psum_scatter(v.reshape(EXPERTS * 2 * part, width), 'dp', scatter_dime...]
    reduce_scatter x1, waiting for transfers between devices: 60.4 us -> 15.3 us  [plane_body(): lax.psum_scatter(gwa, both, scatter_dimension=0, tiled=True)]
    all_to_all x1 -> x0, blocking collectives: 17.3 us -> none  [plane_body(): w1 = lax.all_to_all(w_in, 'fsdp', split_axis=1, concat_axis=0, tiled=True)]
  transfers between devices with their start and end apart: 11 -> 8, of which waited for: 8 -> 5; matrix products, arithmetic and copies ran while one was open for 1% -> 1% of each run, Pallas kernels for 7% -> 8%
where the time goes in v2:
time: 707 us; the launch traced here: 705 us
  waiting for transfers between devices  322 us (46%)
  Pallas kernels  257 us (36%)
  blocking collectives  83.2 us (12%)
  local copies, waits for them, and re-layouts  18.7 us (3%)
  between operations  14.9 us (2%)
    reduce_scatter x2, waiting for transfers between devices, sum_owners(): lax.psum_scatter(v.reshape(EXPERTS * 2 * part, width), 'dp', scatter_dime...  177 us
    pallas_call x1, Pallas kernels, front(): pl.pallas_call(front_kernel, out_shape=(jax.ShapeDtypeStruct((slots, 3 *...  155 us
    reduce_scatter x2, waiting for transfers between devices, plane_body(): lax.psum_scatter(v, 'fsdp', scatter_dimension=0, tiled=True, axis_index_g...  128 us
    pallas_call x1, Pallas kernels, back(): pl.pallas_call(back_kernel, out_shape=(jax.ShapeDtypeStruct((slots, width...  56.6 us
    pallas_call x1, Pallas kernels, experts(): pl.pallas_call(experts_kernel, out_shape=(out_rows, out_rows, jax.ShapeDt...  45.5 us
    psum x1, blocking collectives, plane_body(): expert_counts = lax.psum(counts[:EXPERTS, 0], both)  43.4 us
    unnamed x1, blocking collectives  39.7 us
    reduce_scatter x1, waiting for transfers between devices, plane_body(): lax.psum_scatter(gwa, both, scatter_dimension=0, tiled=True)  15.3 us
  transfers between devices with their start and end apart: 8, of which 5 were waited for; matrix products, arithmetic and copies ran while one was open for 1% of the time, Pallas kernels for 8%

profile of v2, /device:TPU:0, one launch (start us, length us, event | category | flops | bytes accessed | tf_op | source)
XLA Modules:
  0.0 705.2 jit_solution(15162640106581611886)
XLA Ops:
  7.2 0.0 reduce-scatter.15.cloned.1.call-start
  7.2 0.8 slice.34
  8.0 0.9 slice.33
  9.5 0.7 pad_maximum_fusion
  10.2 0.1 copy.30
  10.3 0.8 convert.8
  11.1 0.7 copy.29
  11.8 0.8 fusion.4
  12.6 0.7 pad.15.local_ref
  13.3 155.2 %front.1 = (bf16[1024,2304]{1,0:T(8,128)(2,1)}, bf16[1024,768]{1,0:T(8,128)(2,1)}, bf16[12,1024,128]{2,1,0:T(8,128)(2,1)}, f32[1024,768]{1,0:T(8,128)}, bf16[4,1...) custom-call(s32[1]{0:T(128)S(6)} %copy.34.len_ref, ...), custom_call_target="tpu_custom_call" | custom-call | tf_op jit(solution)/shard_map/front/pallas_call | solution.py:790
  168.5 0.8 convert_reduce_fusion
  169.3 0.6 reshape.62.n_ref
  170.0 8.2 %fusion.5 = (bf16[1,4,2,384,768]{4,3,2,1,0:T(8,128)(2,1)}, bf16[1,4,2,384,768]{4,3,2,1,0:T(8,128)(2,1)}) fusion(bf16[2,4,2,384,768]{4,3,2,1,0:T(8,128)(2,1)} %get-tuple-element.35), kind=kLoop, calls=%fused_computation.13 | loop fusion | bytes 18874368 | tf_op jit(solution)/shard_map/slice | solution.py:1192
  178.2 45.5 %experts.1 = (bf16[4,68,16,768]{3,2,1,0:T(8,128)(2,1)}, bf16[4,68,16,768]{3,2,1,0:T(8,128)(2,1)}, bf16[4,768,768]{2,1,0:T(8,128)(2,1)}, bf16[4,768,768]{2,1,0:T(8,128)(2,1)}) custom-call(s32[16]{0:T(128)} %reshape.62.n_ref, bf16[4,69,16,768]{3,2,1,0:T(8,128)(2,1)} %bitcast.21, bf16[4,69,16,768]{3,2,1,0:T(8,128)(2,1)} %bitcast.22, ...), custom_call_target="tpu_custom_call" | custom-call | tf_op jit(solution)/shard_map/experts/pallas_call | solution.py:1001
  223.7 0.0 reduce-scatter.15.cloned.1.call-update
  223.7 0.0 reduce-scatter.19.cloned.1.call-start
  223.7 0.7 reduce-scatter.19.cloned.1.call-update
  224.4 0.0 reduce-scatter.11.cloned.1.call-start
  224.5 0.7 reduce-scatter.11.cloned.1.call-update
  225.2 0.0 reduce-scatter.9.cloned.1.call-start
  225.2 0.5 reduce-scatter.9.cloned.1.call-update
  225.8 0.0 reduce-scatter.17.cloned.1.call-start
  225.8 89.1 %reduce-scatter.15.cloned.1.call-done = bf16[768,768]{1,0:T(8,128)(2,1)} async-done(((bf16[3072,768]{1,0:T(8,128)(2,1)}), bf16[768,768]{1,0:T(8,128)(2,1)}) %reduce-scatter.15.cloned.1.call-update) | async-done | bytes 1179664 | tf_op jit(solution)/shard_map/reduce_scatter | solution.py:1201
  314.9 0.0 reduce-scatter.17.cloned.1.call-update
  315.0 0.0 reduce-scatter.21.cloned.1.call-start
  315.0 88.0 %reduce-scatter.19.cloned.1.call-done = bf16[768,768]{1,0:T(8,128)(2,1)} async-done(((bf16[3072,768]{1,0:T(8,128)(2,1)}), bf16[768,768]{1,0:T(8,128)(2,1)}) %reduce-scatter.19.cloned.1.call-update) | async-done | bytes 1179664 | tf_op jit(solution)/shard_map/reduce_scatter | solution.py:1201
  403.1 0.0 reduce-scatter.21.cloned.1.call-update
  403.1 0.0 reduce-scatter.13.cloned.1.call-start
  403.1 64.0 %reduce-scatter.11.cloned.1.call-done.os_ref = bf16[1088,768]{1,0:T(8,128)(2,1)} async-done(((bf16[4352,768]{1,0:T(8,128)(2,1)}), bf16[1088,768]{1,0:T(8,128)(2,1)}) %reduce-scatter.11.cloned.1.call-update) | async-done | bytes 1671184 | tf_op jit(solution)/shard_map/reduce_scatter | solution.py:1196
  467.2 63.8 %reduce-scatter.9.cloned.1.call-done.dxs_ref = bf16[1088,768]{1,0:T(8,128)(2,1)} async-done(((bf16[4352,768]{1,0:T(8,128)(2,1)}), bf16[1088,768]{1,0:T(8,128)(2,1)}) %reduce-scatter.9.cloned.1.call-update) | async-done | bytes 1671184 | tf_op jit(solution)/shard_map/reduce_scatter | solution.py:1196
  530.9 56.6 %back.1 = (bf16[1024,768]{1,0:T(8,128)(2,1)}, f32[1024,768]{1,0:T(8,128)}, bf16[768,3072]{1,0:T(8,128)(2,1)}, f32[8,768]{1,0:T(8,128)}) custom-call(s32[1]{0:T(128)S(6)} %copy.34.len_ref, bf16[1024,768]{1,0:T(8,128)(2,1)} %x_ref.3, bf16[1024,768]{1,0:T(8,128)(2,1)} %g_ref.3, f32[1024,768]{1,0:T(8,128)} %get-tuple-element.28.hidden_ref, ...), custom_call_target="tpu_custom_call" | custom-call | tf_op jit(solution)/shard_map/back/pallas_call | solution.py:1141
  587.5 0.0 copy-start.1
  587.5 0.0 reduce-scatter.13.cloned.1.call-update
  587.5 0.0 reduce-scatter.17.cloned.1.call-done
  587.6 0.0 copy-start
  587.6 3.5 all-to-all-start
  591.1 0.0 copy-done.1
  591.1 0.1 slice_reduce_fusion
  591.2 43.4 %psum.7 = s32[4]{0:T(128)} all-reduce(s32[4]{0:T(128)S(1)} %slice_reduce_fusion), channel_id=1, replica_groups=mesh['dp'=4,'fsdp'=8] {'dp','fsdp'}, use_global_device_ids=true, to_apply=%region_8.9 | all-reduce | flops 4 | bytes 32 | tf_op jit(solution)/shard_map/psum | solution.py:1187
  634.6 0.0 reduce-scatter.21.cloned.1.call-done
  634.6 2.2 convert_element_type.43
  636.8 0.0 all-to-all-done
  636.8 0.6 reshape.64
  637.4 0.8 copy.31
  638.2 1.5 reshape.63
  639.7 0.0 copy-done
  639.7 39.7 %all-reduce.3 = f32[768,4]{0,1:T(4,128)S(1)} all-reduce(f32[768,4]{0,1:T(4,128)S(1)} %slice_bitcast_fusion), channel_id=5, replica_groups=mesh['dp'=4,'fsdp'=8] {'dp','fsdp'}, use_global_device_ids=true, to_apply=%region_3.4.clone | all-reduce | flops 3072 | bytes 24576
  679.4 0.1 constant_dynamic-slice_fusion
  679.5 0.6 fusion.6
  680.1 15.3 %reduce-scatter.13.cloned.1.call-done = bf16[24,3072]{1,0:T(8,128)(2,1)} async-done(((bf16[768,3072]{1,0:T(8,128)(2,1)}), bf16[24,3072]{1,0:T(8,128)(2,1)}) %reduce-scatter.13.cloned.1.call-update) | async-done | bytes 147472 | tf_op jit(solution)/shard_map/reduce_scatter | solution.py:1211
  695.4 1.4 slice.46
  696.8 1.6 slice.45
  (2 shorter events, 0.0 us)
Async XLA Ops:
  7.2 307.8 %reduce-scatter.15.cloned.1.call-start = ((), (), s32[]{:S(2)}) async-start(), calls=%async_computation.11 | async-start | bytes 5898240 | tf_op jit(solution)/shard_map/reduce_scatter | solution.py:1201
  223.7 179.4 %reduce-scatter.19.cloned.1.call-start = ((), (), s32[]{:S(2)}) async-start(), calls=%async_computation.13 | async-start | bytes 5898240 | tf_op jit(solution)/shard_map/reduce_scatter | solution.py:1201
  224.4 242.7 %reduce-scatter.11.cloned.1.call-start = ((), (), s32[]{:S(2)}) async-start(), calls=%async_computation.9 | async-start | bytes 8355840 | tf_op jit(solution)/shard_map/reduce_scatter | solution.py:1196
  225.2 305.7 %reduce-scatter.9.cloned.1.call-start = ((), (), s32[]{:S(2)}) async-start(), calls=%async_computation.8 | async-start | bytes 8355840 | tf_op jit(solution)/shard_map/reduce_scatter | solution.py:1196
  225.8 361.8 %reduce-scatter.17.cloned.1.call-start = ((), (), s32[]{:S(2)}) async-start(), calls=%async_computation.12 | async-start | bytes 1769472 | tf_op jit(solution)/shard_map/reduce_scatter | solution.py:1202
  315.0 319.6 %reduce-scatter.21.cloned.1.call-start = ((), (), s32[]{:S(2)}) async-start(), calls=%async_computation.14 | async-start | bytes 1769472 | tf_op jit(solution)/shard_map/reduce_scatter | solution.py:1202
  403.1 292.3 %reduce-scatter.13.cloned.1.call-start = ((), (), s32[]{:S(2)}) async-start(), calls=%async_computation.10 | async-start | bytes 4866048 | tf_op jit(solution)/shard_map/reduce_scatter | solution.py:1211
  587.5 3.6 copy-start.1
  587.6 52.1 %copy-start = (f32[8,768]{1,0:T(8,128)S(1)}, f32[8,768]{1,0:T(8,128)}, u32[]{:S(2)}) copy-start(f32[8,768]{1,0:T(8,128)} %get-tuple-element.43) | copy-start | bytes 73732
  587.6 49.2 %all-to-all-start = ((bf16[4,96,768]{2,1,0:T(8,128)(2,1)}), bf16[4,96,768]{2,1,0:T(8,128)(2,1)S(1)}, u32[]{:S(2)}, u32[]{:S(2)}) async-start(bf16[4,96,768]{2,1,0:T(8,128)(2,1)} %bitcast.28), calls=%async_computation.5 | async-start | bytes 1179648 | tf_op jit(solution)/shard_map/all_to_all | solution.py:1206
Sparse Core Ops, SparseCore 0:
  223.8 91.0 reduce-scatter.14
  317.2 85.7 reduce-scatter.18
  405.6 61.4 reduce-scatter.10
  469.7 61.1 reduce-scatter.8
  533.0 21.7 reduce-scatter.16
  557.0 21.7 reduce-scatter.20
  587.6 107.6 reduce-scatter.12

commit v3 on v2

--- a/solution.py
+++ b/solution.py
@@ -827,13 +827,12 @@
 
 
 def experts_kernel(
-    n_ref, x_ref, g_ref, w1_ref, w2_ref,
+    n_ref, x_ref, g_ref, w_ref,
     o_ref, dx_ref, gw1_ref, gw2_ref,
     xb, gb, ob, db, acc1, acc2, blank, sem_in, sem_out, sem_zero,
 ):
     sources, groups, _, width = x_ref.shape
     groups = groups - 1
-    hidden = w2_ref.shape[1]
     rows = CHUNK * GROUP
 
     blank[...] = jnp.zeros_like(blank)
@@ -949,8 +948,8 @@
         x = xb[slot].reshape(rows, width)
         g = gb[slot].reshape(rows, width)
         g = jnp.where(iota((rows, width), 0) < (end - begin) * GROUP, g, jnp.zeros_like(g))
-        w1 = w1_ref[e]
-        w2 = w2_ref[e]
+        w1 = w_ref[0, e]
+        w2 = w_ref[1, e]
         pre = mul(x, w1)
         square = pre * pre
         t = jnp.tanh(ROOT * pre * (1.0 + CUBIC * square))
@@ -991,9 +990,9 @@
         rest(s, lambda copy: copy.wait())
 
 
-def experts(n16, xs, gs, w1, w2):
+def experts(n16, xs, gs, w):
     sources, groups, _, width = xs.shape
-    hidden = w2.shape[1]
+    hidden = w.shape[2]
     bf = jnp.bfloat16
     whole = pl.BlockSpec(memory_space=pltpu.VMEM)
     far = pl.BlockSpec(memory_space=pl.ANY)
@@ -1005,7 +1004,7 @@
             jax.ShapeDtypeStruct((EXPERTS, width, hidden), bf),
             jax.ShapeDtypeStruct((EXPERTS, hidden, width), bf),
         ),
-        in_specs=[pl.BlockSpec(memory_space=pltpu.SMEM), far, far, whole, whole],
+        in_specs=[pl.BlockSpec(memory_space=pltpu.SMEM), far, far, whole],
         out_specs=(far, far, whole, whole),
         scratch_shapes=[pltpu.VMEM((2, CHUNK, GROUP, width), bf)] * 4
         + [pltpu.VMEM((width, hidden), jnp.float32), pltpu.VMEM((hidden, width), jnp.float32)]
@@ -1013,59 +1012,506 @@
         + [pltpu.SemaphoreType.DMA((2, 2)), pltpu.SemaphoreType.DMA((2, 2)), pltpu.SemaphoreType.DMA((2, sources))],
         compiler_params=pltpu.CompilerParams(vmem_limit_bytes=56 * MIB),
         name="experts",
-    )(n16, xs, gs, w1, w2)
+    )(n16, xs, gs, w)
+
+
+GROUPS = 4
+UNIT = 384
 
 
 def back_kernel(
-    len_ref, x_ref, g_ref, hidden_ref, qkv_ref, mixed_ref, aug_ref, pos_ref, dxs_ref, os_ref, wa_ref, norms_ref,
-    out_ref, gx_ref, gwa_ref, gn_ref,
-    branch_ref, gmix_ref, gqkv_ref, tr_ref, qa_ref, ka_ref, va_ref, oa_ref, dv_ref, dk_ref, dq_ref,
+    len_ref, norms_ref, counts_ref, x_far, g_far, hidden_far, qkv_far, mixed_far, aug_far, pos_far, wa_far,
+    o_far, dx_far, gw1_far, gw2_far,
+    out_far, gx_far, gwq_ref, gwo_ref, gn_out, cnt_out, gwin_ref, gwout_ref,
+    y_land, up_land, down_land, o_near, o_beside,
+    x_ref, g_ref, gx_ref, qkv_ref, mixed_ref, aug_ref, pos_ref, wa_ref,
+    branch_ref, gmix_ref, first_t, mixed_t,
+    qa_ref, ka_ref, va_ref, oa_ref, dv_ref, dk_ref, dq_ref,
+    dx_own, dx_near, dx_beside, os_ref, in_ref, sum_ref, lane_out, lane_in, hid_ref, outb_ref,
+    half_land, d_land, y_small, x_small, z_small, last_out, last_in,
+    gn_ref, gn_send, gn_land, gn_t,
+    load_sem, aug_sem, dxs_send, dxs_recv, dxx_send, dxx_recv,
+    yw_send, yw_recv, up_send, up_recv, dn_send, dn_recv, on_send, on_recv, ob_send, ob_recv, in_sem,
+    ln_send, ln_recv, h_send, h_recv, d_send, d_recv, sy_send, sy_recv, sx_send, sx_recv, sz_send, sz_recv,
+    l_send, l_recv, gs_send, gs_recv, hid_sem, out_sem, gx_sem,
 ):
     slots, width = x_ref.shape
     heads = width // HEAD_DIM
-    rp = dxs_ref.shape[0]
+    pairs = heads // 2
+    rp = dx_own.shape[1]
+    piece = rp // 4
+    part = gw1_far.shape[2]
+    owned = gwq_ref.shape[0]
+    depth = 4
     length = len_ref[0]
     scale = HEAD_DIM ** -0.5
+    f32 = jnp.float32
+    bf = jnp.bfloat16
+    me = Place()
+    z, y, x, c = me.z, me.y, me.x, me.c
+    sibling, beside, across = me.at(c=1 - c), me.at(x=1 - x), me.at(y=1 - y)
+    above, below = me.at(z=jnp.minimum(z + 1, depth - 1)), me.at(z=jnp.maximum(z - 1, 0))
+    me.greet([sibling, beside, across, me.at(x=1 - x, c=1 - c)] + [me.at(z=z ^ k) for k in range(1, depth)])
+
+    loads = {
+        "dx": [pltpu.make_async_copy(dx_far.at[2 * xx + c], dx_own.at[xx], load_sem.at[xx]) for xx in range(2)],
+    }
+    plain = (
+        ("x", x_far, x_ref), ("mixed", mixed_far, mixed_ref), ("hidden", hidden_far, gx_ref), ("g", g_far, g_ref),
+        ("pos", pos_far, pos_ref), ("wa", wa_far, wa_ref), ("qkv", qkv_far, qkv_ref),
+    )
+    for i, (name, src, dst) in enumerate(plain):
+        loads[name] = [pltpu.make_async_copy(src, dst, load_sem.at[2 + i])]
+
+    def loaded(*names):
+        for name in names:
+            for copy in loads[name]:
+                copy.wait()
+
+    def dx_sib(xx):
+        return push(dx_far.at[2 * xx + 1 - c], dx_near.at[xx], dxs_send.at[xx], dxs_recv.at[xx], sibling)
+
+    def rows_of(i):
+        return pl.ds(i * piece, piece)
+
+    def dx_over(i):
+        return push(dx_own.at[1 - x, rows_of(i)], dx_beside.at[rows_of(i)], dxx_send.at[i], dxx_recv.at[i], beside)
+
+    gws = (gw1_far, gw2_far)
+
+    def y_push(k, e):
+        return push(gws[k].at[e, 1 - y], y_land.at[k, e], yw_send.at[k, e], yw_recv.at[k, e], across)
+
+    def up_push(k, e, slot):
+        return push(sum_ref.at[slot], up_land.at[k, e], up_send.at[k, e], up_recv.at[k, e], above)
+
+    def down_push(k, e, slot):
+        return push(sum_ref.at[slot], down_land.at[k, e], dn_send.at[k, e], dn_recv.at[k, e], below)
+
+    def o_sib(xx):
+        return push(o_far.at[2 * xx + 1 - c], o_near.at[xx], on_send.at[xx], on_recv.at[xx], sibling)
+
+    def o_over(i, slot):
+        return push(sum_ref.at[slot, pl.ds(0, piece)], o_beside.at[rows_of(i)], ob_send.at[i], ob_recv.at[i], beside)
+
+    lanes = [(1 - x, c), (x, 1 - c), (1 - x, 1 - c)]
+    lane_rows = part // 4
+    mine = 2 * x + c
+
+    def lane_push(i, arrive):
+        xx, cc = lanes[i]
+        src = lane_out.at[pl.ds(pl.multiple_of(lane_rows * (2 * xx + cc), 16), lane_rows)]
+        dst = lane_in.at[2 * xx + cc] if arrive else lane_in.at[mine]
+        return push(src, dst, ln_send.at[i], ln_recv.at[i], me.at(x=xx, c=cc))
+
+    weights = [(k, i) for i in range(depth) for k in (0, 1)]
+
+    class WeightItem:
+        def __init__(self, k, i):
+            self.k, self.m = k, 3 - i
+            self.rows = part
+
+        def e(self):
+            return z ^ self.m
+
+        def flags(self):
+            e = self.e()
+            if self.m == 0:
+                return z > 0, z < depth - 1
+            return (e > z) & (z > 0), (e < z) & (z < depth - 1)
+
+        def ready(self):
+            k, e = self.k, self.e()
+            y_push(k, e).wait_recv()
+            for flag, copy in zip(self.flags(), (up_push, down_push)):
+                @pl.when(flag)
+                def _():
+                    copy(k, e, 0).wait_recv()
+
+        def sources(self):
+            k, e = self.k, self.e()
+            a, b = self.flags()
+            return [
+                (gws[k].at[e, y], None), (y_land.at[k, e], None), (up_land.at[k, e], a), (down_land.at[k, e], b)
+            ]
+
+        def finish(self, total, slot):
+            k, e = self.k, self.e()
+            if self.m:
+                def put(rows, value):
+                    sum_ref[slot, rows, :] = value.astype(bf)
+
+                total(put)
+
+                @pl.when(e > z)
+                def _():
+                    up_push(k, e, slot).start()
+
+                @pl.when(e < z)
+                def _():
+                    down_push(k, e, slot).start()
+            elif k == 1:
+                def put(rows, value):
+                    gwout_ref[rows, :] = value
+
+                total(put)
+            else:
+                def put(rows, value):
+                    lane_out[rows, :] = value.astype(bf)
+
+                total(put)
+                for i in range(3):
+                    lane_push(i, False).start()
+                lane_in[mine] = lane_out[pl.ds(pl.multiple_of(lane_rows * mine, 16), lane_rows), :]
+
+        def sent(self, slot):
+            k, e = self.k, self.e()
+            if self.m:
+                @pl.when(e > z)
+                def _():
+                    up_push(k, e, slot).wait_send()
+
+                @pl.when(e < z)
+                def _():
+                    down_push(k, e, slot).wait_send()
+
+    class OutItem:
+        def __init__(self, stage, i):
+            self.stage, self.i = stage, i
+            self.rows = piece
+
+        def ready(self):
+            if self.i == 0:
+                o_sib(1 - x if self.stage == 0 else x).wait_recv()
+            if self.stage:
+                o_over(self.i, 0).wait_recv()
+
+        def sources(self):
+            xx = 1 - x if self.stage == 0 else x
+            rows = rows_of(self.i)
+            found = [(o_far.at[2 * xx + c, rows], None), (o_near.at[xx, rows], None)]
+            if self.stage:
+                found.append((o_beside.at[rows], None))
+            return found
+
+        def finish(self, total, slot):
+            if self.stage == 0:
+                def put(rows, value):
+                    sum_ref[slot, rows, :] = value.astype(bf)
+
+                total(put)
+                o_over(self.i, slot).start()
+            else:
+                base = self.i * piece
+
+                def put(rows, value):
+                    os_ref[pl.ds(base + rows.start, rows.size), :] = value.astype(bf)
+
+                total(put)
+
+        def sent(self, slot):
+            if self.stage == 0:
+                o_over(self.i, slot).wait_send()
+
+    w_items = [WeightItem(k, i) for k, i in [(kk, ii) for ii in range(depth) for kk in (0, 1)]]
+    o_items = [OutItem(s, i) for s in range(2) for i in range(4)]
+    order = [
+        w_items[0], w_items[1], o_items[0], o_items[1], w_items[2], o_items[2], o_items[3], w_items[3],
+        o_items[4], o_items[5], w_items[4], o_items[6], o_items[7], w_items[5], w_items[6], w_items[7],
+    ]
+    senders = [item for item in order if (isinstance(item, WeightItem) and item.m) or getattr(item, "stage", 1) == 0]
+    sum_slot = {id(item): n % 3 for n, item in enumerate(senders)}
+    state = {"next": 0, "y": 0}
+
+    def y_next():
+        if state["y"] < len(w_items):
+            item = w_items[state["y"]]
+            y_push(item.k, item.e()).start()
+            state["y"] += 1
+
+    def fetch(item, slot):
+        for n, (src, flag) in enumerate(item.sources()):
+            copy = pltpu.make_async_copy(src, in_ref.at[slot, n, pl.ds(0, item.rows)], in_sem.at[slot, n])
+            if flag is None:
+                copy.start()
+            else:
+                pl.when(flag)(copy.start)
+
+    def finish(item, slot):
+        sources = item.sources()
+        for n, (src, flag) in enumerate(sources):
+            copy = pltpu.make_async_copy(src, in_ref.at[slot, n, pl.ds(0, item.rows)], in_sem.at[slot, n])
+            if flag is None:
+                copy.wait()
+            else:
+                pl.when(flag)(copy.wait)
+        place = sum_slot.get(id(item), 0)
+        if id(item) in sum_slot:
+            n = senders.index(item)
+            if n >= 3:
+                senders[n - 3].sent(place)
+
+        tile = 16
+
+        def total(put):
+            @pl.loop(0, item.rows // tile)
+            def _(i):
+                rows = pl.ds(pl.multiple_of(i * tile, tile), tile)
+                value = None
+                for n, (src, flag) in enumerate(sources):
+                    term = in_ref[slot, n, rows, :].astype(f32)
+                    if flag is not None:
+                        term = jnp.where(flag, term, 0.0)
+                    value = term if value is None else value + term
+                put(rows, value)
+
+        item.finish(total, place)
+
+    def tick():
+        n = state["next"]
+        if n > len(order):
+            return
+        if n < len(order):
+            order[n].ready()
+            fetch(order[n], n % 2)
+            if isinstance(order[n], WeightItem):
+                y_next()
+        if n > 0:
+            finish(order[n - 1], (n - 1) % 2)
+        state["next"] += 1
+
+    def home(g, side):
+        store = dx_own if g < 2 else dx_near
+        return store, side, pl.ds((g % 2) * UNIT, UNIT)
+
+    def put_unit(g, u, value):
+        store, side, _ = home(g, u // 3)
+        lo = (g % 2) * UNIT + (u % 3) * 128
+        store[side, 0:width, lo : lo + 128] = value.astype(bf)
+
+    def block_rows(zz, yy, xx):
+        return pl.ds(pl.multiple_of(2 * owned * (4 * zz + 2 * yy + xx), 16), 2 * owned)
+
+    def block(g, zz, yy, xx):
+        store, _, cols = home(g, 0)
+        return store.at[c, block_rows(zz, yy, xx), cols]
+
+    def half_push(g):
+        store, _, cols = home(g, 0)
+        return push(store.at[1 - c, pl.ds(0, width), cols], half_land.at[g], h_send.at[g], h_recv.at[g], sibling)
+
+    def d_push(g, zz, peer):
+        return push(block(g, zz, 1 - y, 1 - x), d_land.at[g, zz], d_send.at[g, zz], d_recv.at[g, zz], peer)
+
+    def ys_push(g, zz):
+        return push(block(g, zz, 1 - y, x), y_small.at[g, zz], sy_send.at[g, zz], sy_recv.at[g, zz], across)
+
+    def xs_push(g, zz):
+        return push(block(g, zz, y, 1 - x), x_small.at[g, zz], sx_send.at[g, zz], sx_recv.at[g, zz], beside)
+
+    def zs_push(g, k, source):
+        zz = z ^ k
+        return push(block(g, zz, y, x), z_small.at[g, source], sz_send.at[g, k - 1], sz_recv.at[g, source], me.at(z=zz))
+
+    def last_push(g):
+        return push(last_out.at[g], last_in.at[g], l_send.at[g], l_recv.at[g], sibling)
+
+    def small_a(g):
+        half_push(g).wait_recv()
+        store, _, cols = home(g, 0)
+
+        @pl.loop(0, width // 64)
+        def _(i):
+            rows = pl.ds(pl.multiple_of(i * 64, 64), 64)
+            store[c, rows, cols] = (store[c, rows, cols].astype(f32) + half_land[g, rows, :].astype(f32)).astype(bf)
+
+        for zz in range(depth):
+            d_push(g, zz, beside if zz % 2 == 0 else across).start()
+
+    def small_b(g):
+        store, _, cols = home(g, 0)
+        for zz in range(depth):
+            d_push(g, zz, beside).wait_recv()
+            rows = block_rows(zz, 1 - y, x) if zz % 2 == 0 else block_rows(zz, y, 1 - x)
+            store[c, rows, cols] = (store[c, rows, cols].astype(f32) + d_land[g, zz].astype(f32)).astype(bf)
+            ys_push(g, zz).start()
+            xs_push(g, zz).start()
+
+    def small_c(g):
+        store, _, cols = home(g, 0)
+        for k in (3, 2, 1, 0):
+            zz = z ^ k
+            ys_push(g, zz).wait_recv()
+            xs_push(g, zz).wait_recv()
+            rows = block_rows(zz, y, x)
+            value = store[c, rows, cols].astype(f32) + y_small[g, zz].astype(f32) + x_small[g, zz].astype(f32)
+            store[c, rows, cols] = value.astype(bf)
+            if k:
+                zs_push(g, k, z).start()
+
+    def columns(g, side):
+        if g == 0:
+            return [(gwo_ref, side * UNIT + 128 * i) for i in range(3)]
+        found = []
+        for i in range(3):
+            u = 3 * side + i
+            found.append((gwq_ref, (u // 2) * width + 256 * (g - 1) + (u % 2) * 128))
+        return found
+
+    def place_columns(g, side, value):
+        for i, (ref, lo) in enumerate(columns(g, side)):
+            ref[:, lo : lo + 128] = value[:, 128 * i : 128 * i + 128]
+
+    def small_d(g):
+        store, _, cols = home(g, 0)
+        for k in range(1, depth):
+            zs_push(g, k, z ^ k).wait_recv()
+        value = store[c, block_rows(z, y, x), cols].astype(f32)
+        for k in range(1, depth):
+            value = value + z_small[g, z ^ k].astype(f32)
+        own_part = jnp.where(c == 0, value[0:owned], value[owned:])
+        last_out[g] = jnp.where(c == 0, value[owned:], value[0:owned])
+        last_push(g).start()
+        for side in range(2):
+            @pl.when(c == side)
+            def _():
+                place_columns(g, side, own_part)
+
+    def small_e(g):
+        last_push(g).wait_recv()
+        for side in range(2):
+            @pl.when(c != side)
+            def _():
+                place_columns(g, side, last_in[g])
+
+    def small_end(g):
+        half_push(g).wait_send()
+        for zz in range(depth):
+            d_push(g, zz, beside).wait_send()
+            ys_push(g, zz).wait_send()
+            xs_push(g, zz).wait_send()
+        for k in range(1, depth):
+            zs_push(g, k, z).wait_send()
+        last_push(g).wait_send()
+
+    for xx in range(2):
+        dx_sib(xx).start()
+    for name in ("dx", "x", "mixed", "hidden", "g", "pos", "wa", "qkv"):
+        for copy in loads[name]:
+            copy.start()
     gn_ref[...] = jnp.zeros_like(gn_ref)
+    in_ref[...] = jnp.zeros_like(in_ref)
+    dx_sib(1 - x).wait_recv()
+    loaded("dx")
+    for i in range(4):
+        rows = rows_of(i)
+        dx_own[1 - x, rows, :] = (dx_own[1 - x, rows, :].astype(f32) + dx_near[1 - x, rows, :].astype(f32)).astype(bf)
+        dx_over(i).start()
+    for _ in range(3):
+        y_next()
+    for xx in range(2):
+        o_sib(xx).start()
+
+    loaded("x", "mixed")
+
+    @pl.loop(0, slots // ROWS)
+    def _(i):
+        rows = pl.ds(i * ROWS, ROWS)
+        normal, _ = layer_stats(x_ref[rows, :].astype(f32))
+        branch_ref[rows, :] = (normal * norms_ref[0:1, :] + norms_ref[2:3, :]).astype(bf)
+
+    first_t[...] = branch_ref[...].T
+    mixed_t[...] = mixed_ref[...].T
+    loaded("hidden", "g", "pos", "wa", "qkv")
+    dx_sib(x).wait_recv()
+    for i in range(4):
+        rows = rows_of(i)
+        dx_over(i).wait_recv()
+        dx_own[x, rows, :] = (
+            dx_own[x, rows, :].astype(f32) + dx_near[x, rows, :].astype(f32) + dx_beside[rows, :].astype(f32)
+        ).astype(bf)
 
     @pl.loop(0, slots // ROWS)
     def _(i):
         rows = pl.ds(i * ROWS, ROWS)
         place = pos_ref[rows, 0:1].astype(jnp.int32)
-        pick = (iota((ROWS, rp), 1) == place).astype(jnp.bfloat16)
-        hidden = hidden_ref[rows, :]
-        out_ref[rows, :] = (hidden + mul(pick, os_ref[...])).astype(jnp.bfloat16)
-        grad = mul(pick, dxs_ref[...])
-        normal, scaled = layer_stats(hidden)
+        pick = (iota((ROWS, rp), 1) == place).astype(bf)
+        grad = mul(pick, dx_own[x])
+        normal, scaled = layer_stats(gx_ref[rows, :])
         gn_ref[1:2, :] += jnp.sum(grad * normal, axis=0, keepdims=True)
         gn_ref[3:4, :] += jnp.sum(grad, axis=0, keepdims=True)
-        grad_hidden = g_ref[rows, :].astype(jnp.float32) + norm_backward(grad, normal, scaled, norms_ref[1:2, :])
+        grad_hidden = g_ref[rows, :].astype(f32) + norm_backward(grad, normal, scaled, norms_ref[1:2, :])
         gx_ref[rows, :] = grad_hidden
-        branch = grad_hidden.astype(jnp.bfloat16)
+        branch = grad_hidden.astype(bf)
         branch_ref[rows, :] = branch
-        gmix_ref[rows, :] = mul(branch, wa_ref[:, HALF + width : HALF + 2 * width], NT).astype(jnp.bfloat16)
-
-    tr_ref[...] = mixed_ref[...].T
+        gmix_ref[rows, :] = mul(branch, wa_ref[:, HALF + width : HALF + 2 * width], NT).astype(bf)
+
+    for i in range(4):
+        dx_over(i).wait_send()
     tile = width // 3
 
     @pl.loop(0, 3)
     def _(i):
         rows = pl.ds(i * tile, tile)
-        gwa_ref[rows, 3 * width :] = mul(tr_ref[rows, :], branch_ref[...]).astype(gwa_ref.dtype)
+        value = mul(mixed_t[rows, :], branch_ref[...]).astype(bf)
+        for side in range(2):
+            dx_own[side, rows, 0:UNIT] = value[:, side * UNIT : (side + 1) * UNIT]
+
+    half_push(0).start()
+    tick()
+    tick()
+
+    def group_product(g):
+        j = g - 1
+        store_units = []
+        for t in range(3):
+            lo = t * width + 256 * j
+            for i in range(3):
+                rows = slice(i * tile, (i + 1) * tile)
+                value = mul(first_t[rows, :], qkv_ref[:, lo : lo + 256]).astype(bf)
+                for n in range(2):
+                    u = 2 * t + n
+                    store, side, _ = home(g, u // 3)
+                    at = (g % 2) * UNIT + (u % 3) * 128
+                    store[side, rows, at : at + 128] = value[:, n * 128 : (n + 1) * 128]
+        half_push(g).start()
+
+    plan = [
+        [tick, lambda: small_a(0), tick],
+        [tick, lambda: small_b(0), tick, lambda: group_product(1)],
+        [tick, lambda: small_c(0), lambda: small_a(1), tick],
+        [tick, lambda: small_d(0), lambda: small_b(1), tick, lambda: group_product(2)],
+        [tick, lambda: small_e(0), lambda: small_c(1), lambda: small_a(2), tick],
+        [tick, lambda: small_d(1), lambda: small_b(2), tick, lambda: group_product(3)],
+    ]
 
     lane = iota((slots, 128), 1)
-    key_bias = jnp.where(iota((slots, 128), 0) < length, 0.0, NEGATIVE).astype(jnp.bfloat16)
+    key_bias = jnp.where(iota((slots, 128), 0) < length, 0.0, NEGATIVE).astype(bf)
     causal = iota((ROWS, ROWS), 0) <= iota((ROWS, ROWS), 1)
 
-    @pl.loop(0, heads // 2)
+    def aug_load(p, slot):
+        return pltpu.make_async_copy(aug_far.at[pl.ds(2 * p, 2)], aug_ref.at[slot], aug_sem.at[slot])
+
+    aug_load(0, 0).start()
+
+    @pl.loop(0, pairs)
     def _(p):
+        slot = p % 2
+
+        @pl.when(p + 1 < pairs)
+        def _():
+            aug_load(p + 1, 1 - slot).start()
+
+        aug_load(p, slot).wait()
         cols = pl.ds(p * 128, 128)
+        k_cols = pl.ds(width + p * 128, 128)
+        v_cols = pl.ds(2 * width + p * 128, 128)
         q = qkv_ref[:, cols]
-        q_hi = (q.astype(jnp.float32) * (scale * LOG2E)).astype(jnp.bfloat16)
-        k = qkv_ref[:, pl.ds(width + p * 128, 128)]
-        v = qkv_ref[:, pl.ds(2 * width + p * 128, 128)]
+        q_hi = (q.astype(f32) * (scale * LOG2E)).astype(bf)
+        k = qkv_ref[:, k_cols]
+        v = qkv_ref[:, v_cols]
         do = gmix_ref[:, cols]
-        prod = do.astype(jnp.float32) * mixed_ref[:, cols].astype(jnp.float32)
+        prod = do.astype(f32) * mixed_ref[:, cols].astype(f32)
         k_t = k.T
         zero = jnp.zeros_like(q)
         one = jnp.ones_like(q)
@@ -1074,17 +1520,17 @@
             extra = extra_lane(half)
             parts = (lane > extra) & (lane <= extra + 3)
             qa_ref[half, :, 0:128] = jnp.where(own, q_hi, zero)
-            qa_ref[half, :, 128:256] = aug_ref[2 * p + half]
+            qa_ref[half, :, 128:256] = aug_ref[slot, half]
             ka_ref[half, :, 0:128] = k
             ka_ref[half, :, 128:256] = jnp.where(
                 own, k, jnp.where(lane == extra, key_bias, jnp.where(parts, one, zero))
             )
             va_ref[half, :, :] = jnp.where(own, v, jnp.where(parts, one, zero))
             minus = -jnp.sum(jnp.where(own, prod, 0.0), axis=1, keepdims=True)
-            a, b, c = three_parts(jnp.broadcast_to(minus, (slots, 128)))
+            a, b, d = three_parts(jnp.broadcast_to(minus, (slots, 128)))
             oa_ref[half, :, :] = jnp.where(
                 own, do,
-                jnp.where(lane == extra + 1, a, jnp.where(lane == extra + 2, b, jnp.where(lane == extra + 3, c, zero))),
+                jnp.where(lane == extra + 1, a, jnp.where(lane == extra + 2, b, jnp.where(lane == extra + 3, d, zero))),
             )
         for half in range(2):
             k_own = k_t[half * HEAD_DIM : (half + 1) * HEAD_DIM, :]
@@ -1097,8 +1543,8 @@
                 s = diag if j == slots // ROWS - 1 else jnp.concatenate([diag, s[:, ROWS:]], axis=1)
                 probs = jnp.exp2(s)
                 dp = mul(va_ref[half, keys, :], oa_ref[half, late, :], NT)
-                ds = (probs * dp).astype(jnp.bfloat16)
-                probs = probs.astype(jnp.bfloat16)
+                ds = (probs * dp).astype(bf)
+                probs = probs.astype(bf)
                 dv_ref[half, keys, :] = mul(probs, gmix_ref[late, cols])
                 dk_ref[half, keys, :] = mul(ds, qkv_ref[late, cols])
                 dq = mul(k_own[:, keys], ds)
@@ -1107,63 +1553,167 @@
                 else:
                     dq_ref[heads_rows, late] += dq
         first = lane < HEAD_DIM
-        gqkv_ref[:, cols] = (dq_ref[...].T * scale).astype(jnp.bfloat16)
-        gqkv_ref[:, pl.ds(width + p * 128, 128)] = (jnp.where(first, dk_ref[0], dk_ref[1]) * scale).astype(jnp.bfloat16)
-        gqkv_ref[:, pl.ds(2 * width + p * 128, 128)] = jnp.where(first, dv_ref[0], dv_ref[1]).astype(jnp.bfloat16)
+        qkv_ref[:, cols] = (dq_ref[...].T * scale).astype(bf)
+        qkv_ref[:, k_cols] = (jnp.where(first, dk_ref[0], dk_ref[1]) * scale).astype(bf)
+        qkv_ref[:, v_cols] = jnp.where(first, dv_ref[0], dv_ref[1]).astype(bf)
+        for i in range(pairs):
+            @pl.when(p == i)
+            def _():
+                for step in plan[i]:
+                    step()
 
     @pl.loop(0, slots // ROWS)
     def _(i):
         rows = pl.ds(i * ROWS, ROWS)
-        normal, scaled = layer_stats(x_ref[rows, :].astype(jnp.float32))
-        branch_ref[rows, :] = (normal * norms_ref[0:1, :] + norms_ref[2:3, :]).astype(jnp.bfloat16)
-        grad = mul(gqkv_ref[rows, : 2 * width], wa_ref[:, : 2 * width], NT) + mul(
-            gqkv_ref[rows, 2 * width :], wa_ref[:, HALF : HALF + width], NT
+        normal, scaled = layer_stats(x_ref[rows, :].astype(f32))
+        grad = mul(qkv_ref[rows, : 2 * width], wa_ref[:, : 2 * width], NT) + mul(
+            qkv_ref[rows, 2 * width :], wa_ref[:, HALF : HALF + width], NT
         )
         gn_ref[0:1, :] += jnp.sum(grad * normal, axis=0, keepdims=True)
         gn_ref[2:3, :] += jnp.sum(grad, axis=0, keepdims=True)
         gx_ref[rows, :] += norm_backward(grad, normal, scaled, norms_ref[0:1, :])
 
-    tr_ref[...] = branch_ref[...].T
-
-    @pl.loop(0, 3)
-    def _(i):
-        rows = pl.ds(i * tile, tile)
-        for c in range(3):
-            cols = slice(c * width, (c + 1) * width)
-            gwa_ref[rows, cols] = mul(tr_ref[rows, :], gqkv_ref[:, cols]).astype(gwa_ref.dtype)
-
-
-def back(length, x, g, hidden, qkv, mixed, aug, pos, dxs, os, wa, norms):
+    gx_out = pltpu.make_async_copy(gx_ref, gx_far, gx_sem)
+    gx_out.start()
+    counts = jnp.where(iota((8, 128), 0) == iota((8, 128), 1), counts_ref[...], 0).astype(f32)
+    gn_ref[4:5, 0:128] = jnp.sum(counts, axis=0, keepdims=True)
+    gn_peers = [sibling, beside, across, me.at(z=z ^ 1), me.at(z=z ^ 2)]
+
+    def gn_push(i):
+        return push(gn_send.at[i], gn_land.at[i], gs_send.at[i], gs_recv.at[i], gn_peers[i])
+
+    def gn_start(i):
+        gn_send[i] = gn_ref[...]
+        gn_push(i).start()
+
+    def gn_end(i):
+        gn_push(i).wait_recv()
+        gn_ref[...] += gn_land[i]
+
+    gn_start(0)
+    small_a(3)
+    small_c(2)
+    small_e(1)
+    gn_end(0)
+    gn_start(1)
+    small_b(3)
+    small_d(2)
+    gn_end(1)
+    gn_start(2)
+    while state["next"] <= len(order):
+        tick()
+    gn_end(2)
+    gn_start(3)
+    small_c(3)
+    small_e(2)
+    gn_end(3)
+    gn_start(4)
+
+    def hidden_load(i):
+        return pltpu.make_async_copy(hidden_far.at[pl.ds(i * ROWS, ROWS)], hid_ref.at[i % 2], hid_sem.at[i % 2])
+
+    def out_store(i):
+        return pltpu.make_async_copy(outb_ref.at[i % 2], out_far.at[pl.ds(i * ROWS, ROWS)], out_sem.at[i % 2])
+
+    blocks = slots // ROWS
+    hidden_load(0).start()
+    for i in range(blocks):
+        if i + 1 < blocks:
+            hidden_load(i + 1).start()
+        place = pos_ref[i * ROWS : (i + 1) * ROWS, 0:1].astype(jnp.int32)
+        pick = (iota((ROWS, rp), 1) == place).astype(bf)
+        value = mul(pick, os_ref[...])
+        hidden_load(i).wait()
+        if i >= 2:
+            out_store(i - 2).wait()
+        outb_ref[i % 2] = (hid_ref[i % 2] + value).astype(bf)
+        out_store(i).start()
+
+    gn_end(4)
+    gn_t[...] = jnp.concatenate([gn_ref[...], jnp.zeros((120, width), f32)], axis=0).T
+    gn_out[...] = gn_t[pl.ds(pl.multiple_of(owned * (8 * z + 4 * y + 2 * x + c), 8), owned), :]
+    cnt_out[...] = gn_ref[:, 0:128]
+    small_d(3)
+    for i in range(3):
+        lane_push(i, True).wait_recv()
+    for s in range(4):
+        for b in range(2):
+            lo = (4 * b + s) * part
+            gwin_ref[:, lo : lo + part] = lane_in[s, :, b * part : (b + 1) * part].astype(f32)
+    small_e(3)
+
+    for i in range(blocks - 2, blocks):
+        out_store(i).wait()
+    gx_out.wait()
+    for item in senders[-3:]:
+        item.sent(sum_slot[id(item)])
+    for xx in range(2):
+        dx_sib(xx).wait_send()
+        o_sib(xx).wait_send()
+    for item in w_items:
+        y_push(item.k, item.e()).wait_send()
+    for i in range(3):
+        lane_push(i, False).wait_send()
+    for i in range(5):
+        gn_push(i).wait_send()
+    for g in range(GROUPS):
+        small_end(g)
+
+
+def back(length, norms, counts, x, g, hidden, qkv, mixed, aug, pos, wa, o_part, dx_part, gw1, gw2, owned):
     slots, width = x.shape
+    rp = dx_part.shape[1]
+    part = gw1.shape[2]
     bf = jnp.bfloat16
     f32 = jnp.float32
     whole = pl.BlockSpec(memory_space=pltpu.VMEM)
+    far = pl.BlockSpec(memory_space=pl.ANY)
+    dma = pltpu.SemaphoreType.DMA
+    v = pltpu.VMEM
+    out = jax.ShapeDtypeStruct
     return pl.pallas_call(
         back_kernel,
         out_shape=(
-            jax.ShapeDtypeStruct((slots, width), bf),
-            jax.ShapeDtypeStruct((slots, width), f32),
-            jax.ShapeDtypeStruct((width, 4 * width), bf),
-            jax.ShapeDtypeStruct((8, width), f32),
+            out((slots, width), bf),
+            out((slots, width), f32),
+            out((owned, 3 * width), f32),
+            out((owned, width), f32),
+            out((owned, 128), f32),
+            out((8, 128), f32),
+            out((part // 4, 8 * part), f32),
+            out((part, width), f32),
+            out((2, EXPERTS, part, width), bf),
+            out((2, EXPERTS, part, width), bf),
+            out((2, EXPERTS, part, width), bf),
+            out((2, rp, width), bf),
+            out((rp, width), bf),
         ),
-        in_specs=[pl.BlockSpec(memory_space=pltpu.SMEM)] + [whole] * 11,
-        out_specs=tuple([whole] * 4),
+        in_specs=[pl.BlockSpec(memory_space=pltpu.SMEM), whole, whole] + [far] * 12,
+        out_specs=(far, far, whole, whole, whole, whole, whole, whole, far, far, far, far, far),
         scratch_shapes=[
-            pltpu.VMEM((slots, width), bf),
-            pltpu.VMEM((slots, width), bf),
-            pltpu.VMEM((slots, 3 * width), bf),
-            pltpu.VMEM((width, slots), bf),
-            pltpu.VMEM((2, slots, 256), bf),
-            pltpu.VMEM((2, slots, 256), bf),
-            pltpu.VMEM((2, slots, 128), bf),
-            pltpu.VMEM((2, slots, 128), bf),
-            pltpu.VMEM((2, slots, 128), f32),
-            pltpu.VMEM((2, slots, 128), f32),
-            pltpu.VMEM((128, slots), f32),
+            v((slots, width), bf), v((slots, width), bf), v((slots, width), f32), v((slots, 3 * width), bf),
+            v((slots, width), bf), v((2, 2, slots, 128), bf), v((slots, 128), f32), v((width, WIDE), bf),
+            v((slots, width), bf), v((slots, width), bf), v((width, slots), bf), v((width, slots), bf),
+            v((2, slots, 256), bf), v((2, slots, 256), bf), v((2, slots, 128), bf), v((2, slots, 128), bf),
+            v((2, slots, 128), f32), v((2, slots, 128), f32), v((128, slots), f32),
+            v((2, rp, width), bf), v((2, rp, width), bf), v((rp, width), bf), v((rp, width), bf),
+            v((2, 4, part, width), bf), v((3, part, width), bf), v((part, width), bf), v((4, part // 4, width), bf),
+            v((2, ROWS, width), f32), v((2, ROWS, width), bf),
+            v((GROUPS, width, UNIT), bf),
+            v((GROUPS, 4, 2 * owned, UNIT), bf), v((GROUPS, 4, 2 * owned, UNIT), bf),
+            v((GROUPS, 4, 2 * owned, UNIT), bf), v((GROUPS, 4, 2 * owned, UNIT), bf),
+            v((GROUPS, owned, UNIT), f32), v((GROUPS, owned, UNIT), f32),
+            v((8, width), f32), v((5, 8, width), f32), v((5, 8, width), f32), v((width, 128), f32),
+            dma((9,)), dma((2,)), dma((2,)), dma((2,)), dma((4,)), dma((4,)),
+            dma((2, 4)), dma((2, 4)), dma((2, 4)), dma((2, 4)), dma((2, 4)), dma((2, 4)),
+            dma((2,)), dma((2,)), dma((4,)), dma((4,)), dma((2, 4)),
+            dma((3,)), dma((3,)), dma((4,)), dma((4,)), dma((4, 4)), dma((4, 4)), dma((4, 4)), dma((4, 4)),
+            dma((4, 4)), dma((4, 4)), dma((4, 3)), dma((4, 4)),
+            dma((4,)), dma((4,)), dma((5,)), dma((5,)), dma((2,)), dma((2,)), dma(()),
         ],
-        compiler_params=pltpu.CompilerParams(vmem_limit_bytes=60 * MIB),
+        compiler_params=pltpu.CompilerParams(vmem_limit_bytes=62 * MIB, collective_id=1, has_side_effects=True),
         name="back",
-    )(length, x, g, hidden, qkv, mixed, aug, pos, dxs, os, wa, norms)
+    )(length, norms, counts, x, g, hidden, qkv, mixed, aug, pos, wa, o_part, dx_part, gw1, gw2)
 
 
 def plane_body(
@@ -1171,9 +1721,9 @@
 ):
     slots, width = tokens.shape
     bf = jnp.bfloat16
-    both = ("dp", "fsdp")
     rp = padded_rows(slots)
     part = w_out.shape[0]
+    owned = w_qkv.shape[0]
 
     norm_cols = jnp.concatenate([norm_gains, norm_biases], axis=1)
     local = jnp.concatenate(
@@ -1184,36 +1734,16 @@
     qkv, mixed, aug, hidden, xs, gs, w, wa, norms, pos, counts = front(
         lengths, tokens, token_ids.reshape(1, slots), table, cotangent, local, w_in, w_out
     )
-    expert_counts = lax.psum(counts[:EXPERTS, 0], both)
     xs = xs.reshape(4, rp // GROUP + 1, GROUP, width)
     gs = gs.reshape(4, rp // GROUP + 1, GROUP, width)
     n16 = xs[:, rp // GROUP, :EXPERTS, 0].astype(jnp.int32).reshape(-1)
-    w1 = w[0].reshape(EXPERTS, width, 2 * part)
-    w2 = w[1].reshape(EXPERTS, 2 * part, width)
-    o_part, dx_part, gw1, gw2 = experts(n16, xs, gs, w1, w2)
-    near = [[0, 1, 2, 3], [4, 5, 6, 7]]
-    over = [[0, 4], [1, 5], [2, 6], [3, 7]]
-    sum_near = lambda v: lax.psum_scatter(v, "fsdp", scatter_dimension=0, tiled=True, axis_index_groups=near)
-    os = sum_near(o_part.reshape(4 * rp, width))
-    dxs = sum_near(dx_part.reshape(4 * rp, width))
-
-    def sum_owners(v):
-        v = lax.psum_scatter(v.reshape(EXPERTS * 2 * part, width), "dp", scatter_dimension=0, tiled=True)
-        return lax.psum_scatter(v, "fsdp", scatter_dimension=0, tiled=True, axis_index_groups=over)
-
-    gw1 = sum_owners(gw1)
-    gw2 = sum_owners(gw2)
-    gw1 = lax.all_to_all(
-        gw1.reshape(4, part // 4, 2 * part), "fsdp", split_axis=0, concat_axis=0, tiled=True, axis_index_groups=near
-    )
-    gw1 = gw1.reshape(4, part // 4, 2, part).transpose(1, 2, 0, 3).reshape(part // 4, 8 * part)
-    out, gx, gwa, gn = back(lengths, tokens, cotangent, hidden, qkv, mixed, aug, pos, dxs, os, wa, norms)
-    gwa = lax.psum_scatter(gwa, both, scatter_dimension=0, tiled=True).astype(jnp.float32)
-    gn = lax.psum_scatter(gn[:4].T, both, scatter_dimension=0, tiled=True)
-    return (
-        out, gx, gwa[:, : 3 * width], gwa[:, 3 * width :], gn[:, 0:2], gn[:, 2:4],
-        gw1.astype(jnp.float32), gw2.astype(jnp.float32), expert_counts,
-    )
+    o_part, dx_part, gw1, gw2 = experts(n16, xs, gs, w.reshape(2, EXPERTS, 2 * part, width))
+    out, gx, gwq, gwo, gn, cnt, gwin, gwout = back(
+        lengths, norms, counts, tokens, cotangent, hidden, qkv, mixed, aug, pos, wa,
+        o_part.reshape(4, rp, width), dx_part.reshape(4, rp, width),
+        gw1.reshape(EXPERTS, 2, part, width), gw2.reshape(EXPERTS, 2, part, width), owned,
+    )[:8]
+    return (out, gx, gwq, gwo, gn[:, 0:2], gn[:, 2:4], gwin, gwout, cnt[4, :EXPERTS].astype(jnp.int32))
 
 
 def solution(mesh):

time: 707 us -> 452 us (0.64)
  waiting for transfers between devices: 322 us -> 0 us
  Pallas kernels: 257 us -> 432 us
  blocking collectives: 83.2 us -> 0 us
  between operations: 14.9 us -> 1.35 us
    reduce_scatter x7 -> x0, waiting for transfers between devices: 320 us -> none  [the longest x2 177 us: sum_owners(): lax.psum_scatter(v.reshape(EXPERTS * 2 * part, width), 'dp', scatter_dime...]
    pallas_call x1, Pallas kernels: 56.6 us -> 231 us  [back(): pl.pallas_call(back_kernel, out_shape=(out((slots, width), bf), out((slot...]
    psum x1 -> x0, blocking collectives: 43.4 us -> none  [plane_body(): expert_counts = lax.psum(counts[:EXPERTS, 0], both)]
    unnamed x1 -> x0, blocking collectives: 39.7 us -> none
    slice x4 -> x0, local copies, waits for them, and re-layouts: 11.3 us -> none  [the longest x1 8.2 us: plane_body(): w2 = w[1].reshape(EXPERTS, 2 * part, width)]
    unnamed x5 -> x18, local copies, waits for them, and re-layouts: 0.08 us -> 8.95 us
  transfers between devices with their start and end apart: 8 -> 0, of which waited for: 5 -> 0; matrix products, arithmetic and copies ran while one was open for 1% -> 0% of each run, Pallas kernels for 8% -> 0%
where the time goes in v3:
time: 452 us; the launch traced here: 451 us
  Pallas kernels  432 us (96%)
  local copies, waits for them, and re-layouts  13.6 us (3%)
    pallas_call x1, Pallas kernels, back(): pl.pallas_call(back_kernel, out_shape=(out((slots, width), bf), out((slot...  231 us
    pallas_call x1, Pallas kernels, front(): pl.pallas_call(front_kernel, out_shape=(jax.ShapeDtypeStruct((slots, 3 *...  155 us
    pallas_call x1, Pallas kernels, experts(): pl.pallas_call(experts_kernel, out_shape=(out_rows, out_rows, jax.ShapeDt...  45.6 us

profile of v3, /device:TPU:0, one launch (start us, length us, event | category | flops | bytes accessed | tf_op | source)
XLA Modules:
  0.0 451.5 jit_solution(10280980227530637338)
XLA Ops:
  1.3 0.7 pad_maximum_fusion
  2.0 0.1 copy.30
  2.1 0.8 convert.5
  2.8 0.7 copy.29
  3.6 0.8 slice.19
  4.3 0.9 slice.18
  5.2 0.8 fusion.4
  6.0 0.7 pad.15.local_ref
  6.7 155.3 %front.1 = (bf16[1024,2304]{1,0:T(8,128)(2,1)}, bf16[1024,768]{1,0:T(8,128)(2,1)}, bf16[12,1024,128]{2,1,0:T(8,128)(2,1)}, f32[1024,768]{1,0:T(8,128)}, bf16[4,1...) custom-call(s32[1]{0:T(128)S(6)} %copy.39.len_ref, ...), custom_call_target="tpu_custom_call" | custom-call | tf_op jit(solution)/shard_map/front/pallas_call | solution.py:790
  162.0 0.8 convert_reduce_fusion
  162.9 0.6 reshape.57.n_ref
  163.5 45.6 %experts.1 = (bf16[4,68,16,768]{3,2,1,0:T(8,128)(2,1)}, bf16[4,68,16,768]{3,2,1,0:T(8,128)(2,1)}, bf16[4,768,768]{2,1,0:T(8,128)(2,1)}, bf16[4,768,768]{2,1,0:T(8,128)(2,1)}) custom-call(s32[16]{0:T(128)} %reshape.57.n_ref, bf16[4,69,16,768]{3,2,1,0:T(8,128)(2,1)} %bitcast.15, bf16[4,69,16,768]{3,2,1,0:T(8,128)(2,1)} %bitcast.16, ...), custom_call_target="tpu_custom_call" | custom-call | tf_op jit(solution)/shard_map/experts/pallas_call | solution.py:1000
  209.0 231.3 %back.1 = (bf16[1024,768]{1,0:T(8,128)(2,1)}, f32[1024,768]{1,0:T(8,128)}, f32[24,2304]{1,0:T(8,128)}, f32[24,768]{1,0:T(8,128)}, f32[24,128]{1,0:T(8,128)}, /*i...) custom-call(s32[1]{0:T(128)S(6)} %copy.39.len_ref, ...), custom_call_target="tpu_custom_call" | custom-call | tf_op jit(solution)/shard_map/back/pallas_call | solution.py:1674
  440.3 0.0 copy-start
  440.3 1.3 convert_bitcast_fusion
  441.7 0.9 fusion.5
  442.5 0.6 copy.32
  443.2 0.6 copy.31
  443.8 2.7 copy.40
  446.4 0.0 copy-done
  446.5 0.0 copy-start.3
  446.5 0.0 copy-start.4
  446.5 0.0 copy-start.2
  446.5 0.0 copy-start.1
  446.5 1.7 copy.41
  448.1 0.0 copy-done.3
  448.1 0.7 copy.42
  448.8 0.0 copy-done.4
  448.8 0.6 copy.43
  449.5 0.0 copy-done.2
  449.5 1.0 copy.44
  450.5 0.0 copy-done.1
  450.5 1.0 copy.45
  (1 shorter events, 0.0 us)
Async XLA Ops:
  440.3 6.1 %copy-start = (f32[1024,768]{1,0:T(8,128)S(1)}, f32[1024,768]{1,0:T(8,128)}, u32[]{:S(2)}) copy-start(f32[1024,768]{1,0:T(8,128)} %get-tuple-element.94) | copy-start | bytes 9437188
  446.5 1.7 copy-start.3
  446.5 2.4 copy-start.4
  446.5 3.0 copy-start.2
  446.5 4.0 copy-start.1
